TPU v7x, 32 devices: a whole 2x2x4 slice. The times are simulated.
32 devices in a mesh: seq: 4 (over y, core), wa: 2 (over x), wb: 4 (over z).
Axes of the slice: x: 2, y: 2, z: 4, core: 2. Of those that a mesh axis runs over, the one named last changes fastest.
Arguments:
- residual: bfloat16 [8, 2048, 768], P(('wa', 'wb'), 'seq'), may hold values from -6 to 6
- cotangent: bfloat16 [8, 2048, 768], P(('wa', 'wb'), 'seq'), may hold values from -6 to 6
- norm_gain: bfloat16 [768], replicated, may hold values from 0.5 to 1.5
- w_zx: bfloat16 [768, 2, 1536], P('wa', None, 'wb'), may hold values from -0.21875 to 0.21875
- w_bc: bfloat16 [768, 2, 128], P('wa'), may hold values from -0.21875 to 0.21875
- w_dt: bfloat16 [768, 24], P('wa', 'wb'), may hold values from -0.21875 to 0.21875
- x_kernel: bfloat16 [4, 1536], P(None, 'wb'), may hold values from -3 to 3
- x_offset: bfloat16 [1536], P('wb'), may hold values from -0.5 to 0.5
- bc_kernel: bfloat16 [4, 2, 128], replicated, may hold values from -3 to 3
- bc_offset: bfloat16 [2, 128], replicated, may hold values from -0.5 to 0.5
- dt_bias: float32 [24], P('wb'), may hold values from -6 to -2
- a_log: float32 [24], P('wb'), may hold values from -2.5 to 2.5
- d_skip: float32 [24], P('wb'), may hold values from 0.5 to 1.5
- gate_gain: bfloat16 [1536], P('wb'), may hold values from 0.5 to 1.5
- w_out: bfloat16 [768, 1536], P('wa', 'wb'), may hold values from -0.15625 to 0.15625
Outputs:
- layer_out: bfloat16 [8, 2048, 768], P(('wa', 'wb'), 'seq')
- input_grad: float32 [8, 2048, 768], P(('wa', 'wb'), 'seq')
- norm_gain_grad: float32 [768], replicated
- w_zx_grad: float32 [768, 2, 1536], P('wa', None, 'wb')
- w_bc_grad: float32 [768, 2, 128], P('wa')
- w_dt_grad: float32 [768, 24], P('wa', 'wb')
- x_kernel_grad: float32 [4, 1536], P(None, 'wb')
- x_offset_grad: float32 [1536], P('wb')
- bc_kernel_grad: float32 [4, 2, 128], replicated
- bc_offset_grad: float32 [2, 128], replicated
- dt_bias_grad: float32 [24], P('wb')
- a_log_grad: float32 [24], P('wb')
- d_skip_grad: float32 [24], P('wb')
- gate_gain_grad: float32 [1536], P('wb')
- w_out_grad: float32 [768, 1536], P('wa', 'wb')
All inputs are finite; a program needn't handle non-finite values.
Results may differ from a plain program's by a relative error of at most 0.03.
Values may be sent and summed in bfloat16 or wider, within the bound.
A program may use at most 192 MiB of HBM per device.

v0:
```python
import jax
import jax.numpy as jnp
from jax import lax
from jax.sharding import PartitionSpec as P

SPAN = 256


EPSILON = 1e-05
PRECISION_HIGH = lax.Precision.HIGHEST


def from_behind(x, axis, by):
    devices = lax.axis_size(axis)
    pairs = [(i, i + by) for i in range(devices) if 0 <= i + by < devices]
    return lax.ppermute(x, axis, pairs)


def carried_in(x, axis, combine, identity, reverse):
    devices, place = (lax.axis_size(axis), lax.axis_index(axis))
    everything = jax.tree.map(lambda part: lax.all_gather(part, axis), x)
    start = jax.tree.map(
        lambda part, zero: jnp.broadcast_to(jnp.asarray(zero, part.dtype), part.shape), x, identity
    )

    def step(k, before):
        at = devices - 1 - k if reverse else k
        reached = at > place if reverse else at < place
        new = combine(before, jax.tree.map(lambda part: part[at], everything))
        return jax.tree.map(lambda a, b: jnp.where(reached, a, b), new, before)

    return lax.fori_loop(0, devices, step, start)


def sigmoid_linear(values):
    return values * jax.nn.sigmoid(values)


def sigmoid_slope(values):
    gate_sig = jax.nn.sigmoid(values)
    return gate_sig * (1.0 + values * (1.0 - gate_sig))


def causal_conv(padded, kernel, offset):
    steps_out = padded.shape[1] - kernel.shape[0] + 1
    summation = offset + kernel[0] * padded[:, 0:steps_out]
    for tap_index in range(1, kernel.shape[0]):
        summation = summation + kernel[tap_index] * padded[:, tap_index : tap_index + steps_out]
    return sigmoid_linear(summation)


def span_scan(x_all, b_all, c_all, dt_all, decay_rate, start_state):
    groups = x_all.shape[0]
    blocks = x_all.shape[1] // SPAN

    def to_blocks(values):
        shaped = values.reshape((groups, blocks, SPAN) + values.shape[2:])
        return jnp.moveaxis(shaped, 1, 0)

    position = jnp.arange(SPAN)
    causal = (position[:, None] >= position[None, :])[None, :, :, None]

    def span_step(carry_state, pieces):
        x_blk, b_blk, c_blk, dt_blk = pieces
        log_decay = jnp.cumsum(dt_blk * decay_rate, axis=1)
        decay_gap = log_decay[:, :, None, :] - log_decay[:, None, :, :]
        decay_mat = jnp.where(causal, jnp.exp(jnp.where(causal, decay_gap, 0.0)), 0.0)
        inner_prod = jnp.einsum("gtn,gsn->gts", c_blk, b_blk, precision=PRECISION_HIGH)
        mix_weight = inner_prod[..., None] * decay_mat * dt_blk[:, None, :, :]
        y_blk = jnp.einsum("gtsh,gshp->gthp", mix_weight, x_blk, precision=PRECISION_HIGH)
        carried = jnp.einsum("gtn,ghpn->gthp", c_blk, carry_state, precision=PRECISION_HIGH)
        y_blk = y_blk + carried * jnp.exp(log_decay)[..., None]
        last_decay = log_decay[:, -1, :]
        tail_weight = jnp.exp(last_decay[:, None, :] - log_decay) * dt_blk
        fresh_state = jnp.einsum(
            "gsh,gshp,gsn->ghpn", tail_weight, x_blk, b_blk, precision=PRECISION_HIGH
        )
        carry_state = carry_state * jnp.exp(last_decay)[:, :, None, None] + fresh_state
        return (carry_state, y_blk)

    final_state, y_blocks = lax.scan(
        jax.checkpoint(span_step),
        start_state,
        (to_blocks(x_all), to_blocks(b_all), to_blocks(c_all), to_blocks(dt_all)),
    )
    y_all = jnp.moveaxis(y_blocks, 0, 1).reshape(x_all.shape)
    return (y_all, final_state)


def piece_totals(input_heads, b_mat, dt_val, decay_rate):
    log_decay = jnp.cumsum(dt_val * decay_rate, axis=1)
    last_decay = log_decay[:, -1, :]
    tail_weight = jnp.exp(last_decay[:, None, :] - log_decay) * dt_val
    fresh_state = jnp.einsum(
        "gsh,gshp,gsn->ghpn", tail_weight, input_heads, b_mat, precision=PRECISION_HIGH
    )
    return (last_decay, fresh_state, log_decay)


def chain_forward(earlier, later):
    return (earlier[0] + later[0], earlier[1] * jnp.exp(later[0])[:, :, None, None] + later[1])


def chain_backward(earlier, later):
    return (earlier[0] + later[0], later[1] + jnp.exp(later[0])[:, :, None, None] * earlier[1])


def gather_rows(values):
    return lax.all_gather(values, "wb", axis=0, tiled=True)


def sum_rows(term_fn, rows):
    return lax.psum_scatter(
        term_fn(jnp.int32(0), rows * lax.axis_size("wb")), "wb", scatter_dimension=0, tiled=True
    )


def head_total(values):
    return lax.psum(values, "wb")


def norm_back(d_scaled, rows_f32, inv_rms):
    return inv_rms * d_scaled - rows_f32 * inv_rms**3 * jnp.mean(
        d_scaled * rows_f32, axis=-1, keepdims=True
    )


def body(
    residual,
    cotangent,
    norm_gain,
    w_zx,
    w_bc,
    w_dt,
    x_kernel,
    x_offset,
    bc_kernel,
    bc_offset,
    dt_bias,
    a_log,
    d_skip,
    gate_gain,
    w_out,
):
    seq_dev, piece_len, model_width = residual.shape
    heads_dev = w_dt.shape[1]
    inner_dev = w_zx.shape[2]
    state_dim = w_bc.shape[2]
    head_dim = inner_dev // heads_dev
    kernel_taps = x_kernel.shape[0]
    weight_band_count = lax.axis_size("wb")
    head_band = lax.axis_index("wb")
    rows_own = model_width // lax.axis_size("wa")
    rows_first = lax.axis_index("wa") * rows_own
    inner_all = inner_dev * weight_band_count
    own_tokens = seq_dev * piece_len
    zx_full, bc_full, dt_full, out_full = (
        lax.all_gather(w_zx, "wa", axis=0, tiled=True),
        lax.all_gather(w_bc, "wa", axis=0, tiled=True),
        lax.all_gather(w_dt, "wa", axis=0, tiled=True),
        lax.all_gather(w_out, "wa", axis=0, tiled=True),
    )
    input_weights = jnp.concatenate(
        [
            zx_full.reshape(model_width, 2 * inner_dev),
            bc_full.reshape(model_width, 2 * state_dim),
            dt_full,
        ],
        axis=1,
    )
    gathered = gather_rows(residual)
    local_seqs = gathered.shape[0]
    tokens = local_seqs * piece_len
    rows_f32 = gathered.reshape(tokens, model_width).astype(jnp.float32)
    inv_rms = lax.rsqrt(jnp.mean(rows_f32 * rows_f32, axis=-1, keepdims=True) + EPSILON)
    gain_f32 = norm_gain.astype(jnp.float32)
    normalized_rows = (rows_f32 * inv_rms * gain_f32).astype(jnp.bfloat16)
    projected_rows = jnp.dot(normalized_rows, input_weights, preferred_element_type=jnp.float32)
    split_dt = 2 * inner_dev + 2 * state_dim
    z_part = projected_rows[:, :inner_dev]
    conv_in = projected_rows[:, inner_dev:split_dt].reshape(
        local_seqs, piece_len, inner_dev + 2 * state_dim
    )
    dt_raw = projected_rows[:, split_dt:].reshape(local_seqs, piece_len, heads_dev)
    edge_rows = from_behind(conv_in[:, piece_len - (kernel_taps - 1) :, :], "seq", 1)
    padded = jnp.concatenate([edge_rows, conv_in], axis=1)
    kernel = jnp.concatenate(
        [
            x_kernel.astype(jnp.float32),
            bc_kernel.reshape(kernel_taps, 2 * state_dim).astype(jnp.float32),
        ],
        axis=1,
    )
    offset = jnp.concatenate(
        [x_offset.astype(jnp.float32), bc_offset.reshape(2 * state_dim).astype(jnp.float32)]
    )
    activated, conv_pull = jax.vjp(causal_conv, padded, kernel, offset)
    input_heads = activated[..., :inner_dev].reshape(local_seqs, piece_len, heads_dev, head_dim)
    b_mat = activated[..., inner_dev : inner_dev + state_dim]
    c_mat = activated[..., inner_dev + state_dim :]
    dt_val = jax.nn.softplus(dt_raw + dt_bias)
    decay_rate = -jnp.exp(a_log)
    totals, fresh_state, log_decay = piece_totals(input_heads, b_mat, dt_val, decay_rate)
    zero_total = jnp.zeros_like(totals)
    zero_state = jnp.zeros_like(fresh_state)
    from_earlier = carried_in(
        (totals, fresh_state), "seq", chain_forward, (zero_total, zero_state), False
    )
    (y_ssm, end_state), ssm_pull = jax.vjp(
        span_scan, input_heads, b_mat, c_mat, dt_val, decay_rate, from_earlier[1]
    )
    y_all = (y_ssm + d_skip[:, None] * input_heads).reshape(tokens, inner_dev)
    gate_val = sigmoid_linear(z_part)
    gated = (y_all * gate_val).astype(jnp.bfloat16)
    gated_f32 = gated.astype(jnp.float32)
    residual_f32 = residual.reshape(own_tokens, model_width).astype(jnp.float32)
    square_sum = head_total(jnp.sum(gated_f32 * gated_f32, axis=-1, keepdims=True))
    inv_gate = lax.rsqrt(square_sum / inner_all + EPSILON)
    gain_two = gate_gain.astype(jnp.float32)
    hidden = (gated_f32 * inv_gate * gain_two).astype(jnp.bfloat16)

    def out_term(row_start, size_rows):
        return lax.dot_general(
            hidden, out_full, (((1,), (1,)), ((), ())), preferred_element_type=jnp.float32
        )

    branch = sum_rows(out_term, own_tokens)
    grad_rows = gather_rows(cotangent).reshape(tokens, model_width)
    d_hidden = jnp.dot(grad_rows, out_full, preferred_element_type=jnp.float32)
    out_grad_part = lax.dot_general(
        grad_rows, hidden, (((0,), (0,)), ((), ())), preferred_element_type=jnp.float32
    )
    gain_grad_part = jnp.sum(d_hidden * gated_f32 * inv_gate, axis=0)
    d_norm = d_hidden * gain_two
    cross_sum = head_total(jnp.sum(d_norm * gated_f32, axis=-1, keepdims=True))
    d_gated = inv_gate * d_norm - gated_f32 * inv_gate**3 * cross_sum / inner_all
    d_back = d_gated.astype(jnp.bfloat16).astype(jnp.float32)
    layer_out = (
        (residual_f32 + branch).astype(jnp.bfloat16).reshape(seq_dev, piece_len, model_width)
    )
    d_y = d_back * gate_val
    d_z = d_back * y_all * sigmoid_slope(z_part)
    d_y4 = d_y.reshape(local_seqs, piece_len, heads_dev, head_dim)
    skip_grad = jnp.sum(d_y4 * input_heads, axis=(0, 1, 3))
    direct = jnp.einsum(
        "glhp,gln,glh->ghpn", d_y4, c_mat, jnp.exp(log_decay), precision=PRECISION_HIGH
    )
    from_later = carried_in((totals, direct), "seq", chain_backward, (zero_total, zero_state), True)
    d_heads, d_bmat, d_cmat, d_dt, d_rate, unused_start = ssm_pull((d_y4, from_later[1]))
    d_heads = d_heads + d_skip[:, None] * d_y4
    d_bc = head_total(jnp.concatenate([d_bmat, d_cmat], axis=-1))
    d_act = jnp.concatenate([d_heads.reshape(local_seqs, piece_len, inner_dev), d_bc], axis=-1)
    d_padded, kernel_grad, offset_grad = conv_pull(d_act)
    from_next = from_behind(
        d_padded[:, : kernel_taps - 1, :].astype(jnp.bfloat16), "seq", -1
    ).astype(jnp.float32)
    d_conv = d_padded[:, kernel_taps - 1 :, :]
    d_conv = jnp.concatenate(
        [
            d_conv[:, : piece_len - (kernel_taps - 1), :],
            d_conv[:, piece_len - (kernel_taps - 1) :, :] + from_next,
        ],
        axis=1,
    )
    d_dt_raw = d_dt * jax.nn.sigmoid(dt_raw + dt_bias)
    d_proj = jnp.concatenate(
        [
            d_z,
            d_conv.reshape(tokens, inner_dev + 2 * state_dim),
            d_dt_raw.reshape(tokens, heads_dev),
        ],
        axis=1,
    ).astype(jnp.bfloat16)
    wide_grad = lax.dot_general(
        normalized_rows, d_proj, (((0,), (0,)), ((), ())), preferred_element_type=jnp.float32
    )
    bc_width = 2 * state_dim // weight_band_count
    cotangent_f32 = cotangent.reshape(own_tokens, model_width).astype(jnp.float32)
    column_index = jnp.arange(input_weights.shape[1])
    in_bc = (column_index >= 2 * inner_dev) & (column_index < split_dt)
    keep_cols = jnp.logical_not(in_bc) | ((column_index - 2 * inner_dev) // bc_width == head_band)
    d_share = jnp.where(keep_cols[None, :], d_proj, jnp.zeros_like(d_proj))
    d_normed = lax.dot_general(
        d_share, input_weights, (((1,), (1,)), ((), ())), preferred_element_type=jnp.float32
    )
    norm_grad_part = head_total(jnp.sum(d_normed * rows_f32 * inv_rms, axis=0))
    d_scaled = d_normed * gain_f32

    def input_term(row_start, size_rows):
        return norm_back(d_scaled, rows_f32, inv_rms)

    input_grad = (sum_rows(input_term, own_tokens) + cotangent_f32).reshape(
        seq_dev, piece_len, model_width
    )
    zx_part = jnp.stack([wide_grad[:, :inner_dev], wide_grad[:, inner_dev : 2 * inner_dev]], axis=1)
    bc_part = wide_grad[:, 2 * inner_dev : split_dt].reshape(model_width, 2, state_dim)
    dt_part = wide_grad[:, split_dt:]
    bias_part = jnp.sum(d_dt_raw, axis=(0, 1))
    summed = lax.psum(
        (
            zx_part,
            bc_part,
            dt_part,
            kernel_grad,
            offset_grad,
            bias_part,
            d_rate * decay_rate,
            skip_grad,
            out_grad_part,
            gain_grad_part,
            norm_grad_part,
        ),
        ("seq", "wa"),
    )
    (
        zx_sum,
        bc_sum,
        dt_sum,
        kernel_sum,
        offset_sum,
        bias_sum,
        log_sum,
        skip_sum,
        out_sum,
        gate_sum,
        norm_sum,
    ) = summed
    zx_grad = lax.dynamic_slice_in_dim(zx_sum, rows_first, rows_own, 0)
    bcw_grad = lax.dynamic_slice_in_dim(bc_sum, rows_first, rows_own, 0)
    dtw_grad = lax.dynamic_slice_in_dim(dt_sum, rows_first, rows_own, 0)
    outw_grad = lax.dynamic_slice_in_dim(out_sum, rows_first, rows_own, 0)
    xker_grad = kernel_sum[:, :inner_dev]
    bcker_grad = kernel_sum[:, inner_dev:].reshape(kernel_taps, 2, state_dim)
    xoff_grad = offset_sum[:inner_dev]
    bcoff_grad = offset_sum[inner_dev:].reshape(2, state_dim)
    return (
        layer_out,
        input_grad,
        norm_sum,
        zx_grad,
        bcw_grad,
        dtw_grad,
        xker_grad,
        xoff_grad,
        bcker_grad,
        bcoff_grad,
        bias_sum,
        log_sum,
        skip_sum,
        gate_sum,
        outw_grad,
    )


def solution(mesh):
    return jax.shard_map(
        body,
        mesh=mesh,
        in_specs=(
            P(("wa", "wb"), "seq", None),
            P(("wa", "wb"), "seq", None),
            P(),
            P("wa", None, "wb"),
            P("wa", None, None),
            P("wa", "wb"),
            P(None, "wb"),
            P("wb"),
            P(),
            P(),
            P("wb"),
            P("wb"),
            P("wb"),
            P("wb"),
            P("wa", "wb"),
        ),
        out_specs=(
            P(("wa", "wb"), "seq", None),
            P(("wa", "wb"), "seq", None),
            P(),
            P("wa", None, "wb"),
            P("wa", None, None),
            P("wa", "wb"),
            P(None, "wb"),
            P("wb"),
            P(),
            P(),
            P("wb"),
            P("wb"),
            P("wb"),
            P("wb"),
            P("wa", "wb"),
        ),
        check_vma=False,
    )
```

profile of v0, /device:TPU:0, one launch (start us, length us, event | category | flops | bytes accessed | tf_op | source)
XLA Modules:
  0.0 1061.3 jit_solution(843404884824188465)
XLA Ops:
  10.1 5.5 all_gather.37
  15.8 9.7 all_gather.36
  28.3 7.0 all-gather.11.cloned.1.call-done
  36.9 65.2 %all-gather.9.cloned.1.call-done = bf16[4,512,768]{2,1,0:T(8,128)(2,1)} async-done(((bf16[1,512,768]{2,1,0:T(8,128)(2,1)}), bf16[4,512,768]{2,1,0:T(8,128)(2,1)}) %all-gather.9.cloned.1.call-update) | async-done | bytes 3145744 | tf_op jit(solution)/shard_map/all_gather | solution.py:109
  105.8 3.6 fusion.142
  115.6 7.2 reduce-window.68
  123.7 6.0 copy.452
  133.3 12.3 %fusion.111 = (f32[4,512,640]{2,1,0:T(8,128)S(1)}, f32[4,512,640]{2,1,0:T(8,128)}) fusion(f32[4,512,640]{2,1,0:T(8,128)} %bitcast.448, f32[640]{0:T(1024)S(1)} %get-tuple-element.1043, f32[4,3,640]{2,1,0:T(4,128)S(1)} %collective-permute-done, f32[640]{0:T(1024)S(1)} %get-tuple-element.1044, f32[640]{0:T(1024)S(1)} %get-tuple-element.1045, ...), kind=kLoop, calls=%fused_computation.167 | loop fusion | flops 19660800 | bytes 15772160 | tf_op jit(solution)/shard_map/jvp()/mul | solution.py:36
  150.8 6.0 fusion.129
  159.4 9.6 all_gather.41
  169.2 5.2 all-gather
  180.9 5.4 reshape_reshape.6
  189.8 4.3 copy.405
  195.2 5.5 while.74
  202.8 49.5 %while.73 = (s32[]{:T(128)}, f32[4,6,64,128]{3,2,1,0:T(8,128)S(1)}, f32[2,4,256,6,64]{2,4,3,1,0:T(8,128)}, f32[2,4,6,64,128]{4,3,2,1,0:T(8,128)}, f32[2,4,256,6]...) while((s32[]{:T(128)}, f32[4,6,64,128]{3,2,1,0:T(8,128)S(1)}, ...), condition=%wide.region_8.9_spmd.clone.clone, body=%wide.region_5.8_spmd.clone.clone.sunk | while | flops 2828814336 | bytes 67223856 | solution.py:81
  202.9 7.2 reduce-window.88
  213.2 9.1 fusion.243
  227.7 7.2 reduce-window.88
  237.9 9.1 fusion.243
  252.3 6.0 copy.406
  258.3 5.7 reshape.427
  264.0 5.2 fusion.117
  269.2 9.5 psum.105
  278.8 6.0 fusion.126
  284.8 9.5 psum.106
  294.3 7.9 multiply_reduce_fusion.8
  302.2 5.2 reshape.431
  307.5 6.7 fusion.127
  314.2 6.1 reshape_reshape.7
  320.4 5.1 copy.467
  325.5 16.3 %all-gather.17.cloned.1.call-done = f32[16,6,64,128]{3,2,1,0:T(8,128)} async-done(((f32[4,6,64,128]{3,2,1,0:T(8,128)}), f32[16,6,64,128]{3,2,1,0:T(8,128)}) %all-gather.17.cloned.1.call-update) | async-done | bytes 3145744 | tf_op jit(solution)/shard_map/all_gather | solution.py:21
  341.7 5.4 while.75
  352.4 241.0 %while.76 = (s32[]{:T(128)}, f32[6]{0:T(128)}, f32[4,6,64,128]{3,2,1,0:T(8,128)S(1)}, f32[2,4,256,6,64]{2,4,3,1,0:T(8,128)}, f32[2,4,256,128]{3,2,1,0:T(8,128)},...) while((s32[]{:T(128)}, f32[6]{0:T(128)}, ...), condition=%wide.region_29.30_spmd.clone, body=%wide.region_16.29_spmd.clone.sunk | while | flops 6681284608 | bytes 99614360 | solution.py:81
  367.8 7.2 reduce-window.91
  382.3 12.6 %fusion.269 = (f32[4,256,6]{1,2,0:T(8,128)S(1)}, f32[4,256,6]{1,2,0:T(8,128)}, f32[4,256,6]{1,2,0:T(8,128)}, f32[4,256,256]{2,1,0:T(8,128)}) fusion(f32[4,256,6]{1,2,0:T(8,128)S(1)} %copy.515, f32[4,256,6]{1,2,0:T(8,128)} %copy.516, f32[4,256,256]{2,1,0:T(8,128)S(1)} %fusion.268, pred[256,256]{1,0:T(8,128)(4,1)S(1)} %bitcast.473, ...), kind=kOutput, calls=%fused_computation.63.clone.1 | convolution fusion | flops 1231271936 | bytes 5431296 | tf_op jit(solution)/shard_map/transpose(jvp())/while/body/eval_jaxpr/checkpoint/gtsh,gshp->gthp/dot_general | solution.py:70
  396.8 4.2 multiply_reduce_fusion.12
  410.9 30.2 %reduce-window.92 = f32[4,6,2,128]{3,2,1,0:T(2,128)S(1)} reduce-window(f32[4,6,2,128]{3,2,1,0:T(2,128)S(1)} %copy.522, f32[]{:T(128)} %constant.207.clone.1..sunk.1), window={size=1x1x1x128 pad=0_0x0_0x0_0x0_127}, to_apply=%region_24.24 | reduce-window | flops 780288 | bytes 49156 | tf_op jit(solution)/shard_map/reduce-window.34
  442.7 4.0 fusion.277
  449.9 4.3 fusion.275
  458.8 7.0 bitcast_dynamic-update-slice_fusion.10
  484.5 7.2 reduce-window.91
  499.1 12.6 %fusion.269 = (f32[4,256,6]{1,2,0:T(8,128)S(1)}, f32[4,256,6]{1,2,0:T(8,128)}, f32[4,256,6]{1,2,0:T(8,128)}, f32[4,256,256]{2,1,0:T(8,128)}) fusion(f32[4,256,6]{1,2,0:T(8,128)S(1)} %copy.515, f32[4,256,6]{1,2,0:T(8,128)} %copy.516, f32[4,256,256]{2,1,0:T(8,128)S(1)} %fusion.268, pred[256,256]{1,0:T(8,128)(4,1)S(1)} %bitcast.473, ...), kind=kOutput, calls=%fused_computation.63.clone.1 | convolution fusion | flops 1231271936 | bytes 5431296 | tf_op jit(solution)/shard_map/transpose(jvp())/while/body/eval_jaxpr/checkpoint/gtsh,gshp->gthp/dot_general | solution.py:70
  513.5 4.2 multiply_reduce_fusion.12
  527.6 30.2 %reduce-window.92 = f32[4,6,2,128]{3,2,1,0:T(2,128)S(1)} reduce-window(f32[4,6,2,128]{3,2,1,0:T(2,128)S(1)} %copy.522, f32[]{:T(128)} %constant.207.clone.1..sunk.1), window={size=1x1x1x128 pad=0_0x0_0x0_0x0_127}, to_apply=%region_24.24 | reduce-window | flops 780288 | bytes 49156 | tf_op jit(solution)/shard_map/reduce-window.34
  559.4 4.0 fusion.277
  566.5 4.3 fusion.275
  575.5 7.0 bitcast_dynamic-update-slice_fusion.10
  603.8 4.4 convolution_bitcast_fusion
  608.6 6.0 copy.413
  614.6 5.5 reshape.432
  620.1 3.6 copy.415
  623.7 4.9 multiply_add_fusion.1
  628.7 55.5 %all-reduce.14.cloned.1.call-done = f32[4,512,256]{2,1,0:T(8,128)} async-done(((f32[4,512,256]{2,1,0:T(8,128)}), f32[4,512,256]{2,1,0:T(8,128)}) %all-reduce.14.cloned.1.call-update) | async-done | bytes 2097168 | tf_op jit(solution)/shard_map/psum | solution.py:119
  684.2 16.8 %multiply_reduce_fusion.6 = (f32[640]{0:T(1024)}, f32[640]{0:T(1024)}, f32[640]{0:T(1024)}, f32[640]{0:T(1024)S(1)}, f32[640]{0:T(1024)}, /*index=5*/f32[4,512,640]{2,1,0:T(8,128)}) fusion(f32[4,512,640]{2,1,0:T(8,128)} %bitcast.449, f32[4,3,640]{2,1,0:T(4,128)S(1)} %copy-done.61, f32[2048,640]{1,0:T(8,128)} %copy.452, ...), kind=kLoop, calls=%fused_computation.164 | loop fusion | flops 28832640 | bytes 26257920 | tf_op jit(solution)/shard_map/transpose(jvp())/reduce_sum | solution.py:48
  701.0 9.8 broadcast_multiply_fusion.1
  710.9 10.5 fusion.164
  730.8 3.7 fusion.132
  741.7 4.8 fusion.144
  748.5 8.9 fusion.106
  763.1 9.7 psum.108
  772.8 27.2 %all-reduce.9 = (f32[768]{0:T(1024)}, f32[768,6]{0,1:T(8,128)S(1)}, f32[4,640]{1,0:T(4,128)S(1)}, f32[640]{0:T(1024)S(1)}, f32[6]{0:T(128)}, /*index=5*/f32[6]{0:T(128)}, f32[6]{0:T(128)}, f32[384]{0:T(512)}) all-reduce(f32[768]{0:T(1024)S(1)} %psum.108, ...), channel_id=1, replica_groups=mesh['seq'=4,'wa'=2,'wb'=4] {'seq','wa'}, use_global_device_ids=true, to_apply=%region_35.36 | all-reduce | flops 8978 | bytes 71824 | tf_op jit(solution)/shard_map/psum | solution.py:299
  803.0 21.8 %all-reduce.16.cloned.1.call-done = (f32[768,2,384]{0,2,1:T(8,128)}, f32[768,2,128]{2,1,0:T(2,128)}, f32[768,384]{0,1:T(8,128)}) async-done(((f32[768,2,384]{0,2,1:T(8,128)}, f32[768,2,128]{2,1,0:T(2,128)}, f32[768,384]{0,1:T(8,128)}), (f32[768,2,384]{0,2,1:T(8,128)}, f32[768,2,128]{2,1,0:T(2,128)}, f32[768,384]{0,1:T(8,128)})) %all-reduce.16.cloned.1.call-update) | async-done | bytes 4325392 | tf_op jit(solution)/shard_map/psum | solution.py:299
  831.2 106.9 %reduce-scatter.3.cloned.1.call-done = f32[512,768]{1,0:T(8,128)} async-done(((f32[2048,768]{1,0:T(8,128)}), f32[512,768]{1,0:T(8,128)}) %reduce-scatter.3.cloned.1.call-update) | async-done | bytes 1572880 | tf_op jit(solution)/shard_map/reduce_scatter | solution.py:113
  940.5 111.3 %reduce-scatter.5.cloned.1.call-done = f32[512,768]{1,0:T(8,128)} async-done(((f32[2048,768]{1,0:T(8,128)}), f32[512,768]{1,0:T(8,128)}) %reduce-scatter.5.cloned.1.call-update) | async-done | bytes 1572880 | tf_op jit(solution)/shard_map/reduce_scatter | solution.py:113
  (539 shorter events, 217.9 us)
Async XLA Ops:
  7.2 28.2 %all-gather.11.cloned.1.call-start = ((), (), s32[]{:S(2)}) async-start(), calls=%async_computation.3 | async-start | bytes 1769472 | tf_op jit(solution)/shard_map/all_gather | solution.py:158
  7.9 94.2 %all-gather.9.cloned.1.call-start = ((), (), s32[]{:S(2)}) async-start(), calls=%async_computation.2 | async-start | bytes 3932160 | tf_op jit(solution)/shard_map/all_gather | solution.py:109
  8.7 186.5 %all-gather.15.cloned.1.call-start = ((), (), s32[]{:S(2)}) async-start(), calls=%async_computation.8 | async-start | bytes 3932160 | tf_op jit(solution)/shard_map/all_gather | solution.py:21
  10.1 94.8 %copy-start.66 = (f32[768]{0:T(1024)}, f32[768]{0:T(1024)S(1)}, u32[]{:S(2)}) copy-start(f32[768]{0:T(1024)S(1)} %convert_element_type.68) | copy-start | bytes 9220
  15.8 89.9 %copy-start.57 = (bf16[768,6]{1,0:T(8,128)(2,1)}, bf16[768,6]{1,0:T(8,128)(2,1)S(1)}, u32[]{:S(2)}) copy-start(bf16[768,6]{1,0:T(8,128)(2,1)S(1)} %copy.387) | copy-start | bytes 27652
  25.6 80.2 %copy-start.48 = (bf16[96,8,2,128]{3,1,2,0:T(8,128)(2,1)}, bf16[96,8,2,128]{3,1,2,0:T(8,128)(2,1)S(1)}, u32[]{:S(2)}) copy-start(bf16[96,8,2,128]{3,1,2,0:T(8,128)(2,1)S(1)} %copy.468) | copy-start | bytes 1179652
  27.1 106.2 %copy-start.68 = (f32[640]{0:T(1024)}, f32[640]{0:T(1024)S(1)}, u32[]{:S(2)}) copy-start(f32[640]{0:T(1024)S(1)} %get-tuple-element.1042) | copy-start | bytes 7684
  27.1 106.2 %copy-start.70 = (f32[640]{0:T(1024)}, f32[640]{0:T(1024)S(1)}, u32[]{:S(2)}) copy-start(f32[640]{0:T(1024)S(1)} %get-tuple-element.1043) | copy-start | bytes 7684
  27.1 106.2 %copy-start.72 = (f32[640]{0:T(1024)}, f32[640]{0:T(1024)S(1)}, u32[]{:S(2)}) copy-start(f32[640]{0:T(1024)S(1)} %get-tuple-element.1044) | copy-start | bytes 7684
  27.1 106.2 %copy-start.74 = (f32[640]{0:T(1024)}, f32[640]{0:T(1024)S(1)}, u32[]{:S(2)}) copy-start(f32[640]{0:T(1024)S(1)} %get-tuple-element.1045) | copy-start | bytes 7684
  36.8 68.9 %copy-start.42 = (bf16[96,8,2,384]{3,1,2,0:T(8,128)(2,1)}, bf16[96,8,2,384]{3,1,2,0:T(8,128)(2,1)S(1)}, u32[]{:S(2)}) copy-start(bf16[96,8,2,384]{3,1,2,0:T(8,128)(2,1)S(1)} %copy.455) | copy-start | bytes 3538948
  130.6 2.7 collective-permute-start
  133.3 12.4 %copy-start.60 = (f32[4,3,640]{2,1,0:T(4,128)}, f32[4,3,640]{2,1,0:T(4,128)S(1)}, u32[]{:S(2)}) copy-start(f32[4,3,640]{2,1,0:T(4,128)S(1)} %collective-permute-done) | copy-start | bytes 92164
  150.8 7.4 copy-start.94
  150.8 7.9 copy-start.95
  150.8 8.7 copy-start.50
  150.8 23.7 %copy-start.58 = (f32[4,512,6]{1,0,2:T(4,128)S(1)}, f32[4,512,6]{1,0,2:T(4,128)}, u32[]{:S(2)}) copy-start(f32[4,512,6]{1,0,2:T(4,128)} %get-tuple-element.1162) | copy-start | bytes 147460
  156.8 122.0 %all-gather.13.cloned.1.call-start = ((), (), s32[]{:S(2)}) async-start(), calls=%async_computation.5 | async-start | bytes 3932160 | tf_op jit(solution)/shard_map/all_gather | solution.py:109
  157.4 184.3 %all-gather.17.cloned.1.call-start = ((), (), s32[]{:S(2)}) async-start(), calls=%async_computation.9 | async-start | bytes 3932160 | tf_op jit(solution)/shard_map/all_gather | solution.py:21
  169.1 109.7 %copy-start.37 = (bf16[768,384]{1,0:T(8,128)(2,1)}, bf16[768,384]{1,0:T(8,128)(2,1)S(1)}, u32[]{:S(2)}) copy-start(bf16[768,384]{1,0:T(8,128)(2,1)S(1)} %all_gather.41) | copy-start | bytes 1769476
  175.5 5.3 copy-start.25
  177.4 8.8 copy-start.16
  213.2 9.1 copy-start.20
  213.2 10.7 %copy-start.23 = (f32[2,4,6,64,128]{4,3,2,1,0:T(8,128)S(1)}, f32[2,4,6,64,128]{4,3,2,1,0:T(8,128)}, u32[]{:S(2)}) copy-start(f32[2,4,6,64,128]{4,3,2,1,0:T(8,128)} %get-tuple-element.1474) | copy-start | bytes 4718596 | tf_op jit(solution)/shard_map/jvp()/while
  237.9 9.1 copy-start.20
  237.9 10.7 %copy-start.23 = (f32[2,4,6,64,128]{4,3,2,1,0:T(8,128)S(1)}, f32[2,4,6,64,128]{4,3,2,1,0:T(8,128)}, u32[]{:S(2)}) copy-start(f32[2,4,6,64,128]{4,3,2,1,0:T(8,128)} %get-tuple-element.1474) | copy-start | bytes 4718596 | tf_op jit(solution)/shard_map/jvp()/while
  258.2 5.7 copy-start.78
  264.0 14.8 %copy-start.76 = (f32[384]{0:T(512)S(1)}, f32[384]{0:T(512)}, u32[]{:S(2)}) copy-start(f32[384]{0:T(512)} %convert_element_type.74) | copy-start | bytes 4612
  269.2 25.1 %copy-start.17 = (bf16[2048,384]{0,1:T(8,128)(2,1)}, bf16[2048,384]{0,1:T(8,128)(2,1)S(1)}, u32[]{:S(2)}) copy-start(bf16[2048,384]{0,1:T(8,128)(2,1)S(1)} %get-tuple-element.1137) | copy-start | bytes 4718596
  278.7 15.6 %copy-start.52 = (f32[2048,1]{0,1:T(1,128)}, f32[2048,1]{0,1:T(1,128)S(1)}, u32[]{:S(2)}) copy-start(f32[2048,1]{0,1:T(1,128)S(1)} %get-tuple-element.1135) | copy-start | bytes 24580
  314.2 370.0 %all-reduce.14.cloned.1.call-start = ((), (), s32[]{:S(2)}) async-start(), calls=%async_computation.6 | async-start | bytes 4194304 | tf_op jit(solution)/shard_map/psum | solution.py:119
  352.6 13.1 %copy-start.64 = (f32[6]{0:T(128)}, f32[6]{0:T(128)S(1)}, u32[]{:S(2)}) copy-start(f32[6]{0:T(128)S(1)} %get-tuple-element.1417) | copy-start | bytes 76 | tf_op jit(solution)/shard_map/transpose(jvp())/while
  352.6 29.7 %copy-start.39 = (pred[1,256,256,1]{2,1,3,0:T(8,128)(4,1)}, pred[1,256,256,1]{2,1,3,0:T(8,128)(4,1)S(1)}, u32[]{:S(2)}) copy-start(pred[1,256,256,1]{2,1,3,0:T(8,128)(4,1)S(1)} %iota_compare_fusion.5) | copy-start | bytes 196612 | tf_op jit(solution)/shard_map/transpose(jvp())/while
  380.3 14.7 %copy-start.44 = (f32[4,256,6]{1,2,0:T(8,128)}, f32[4,256,6]{1,2,0:T(8,128)S(1)}, u32[]{:S(2)}) copy-start(f32[4,256,6]{1,2,0:T(8,128)S(1)} %copy.515) | copy-start | bytes 73732 | tf_op jit(solution)/shard_map/transpose(jvp())/while
  382.3 12.6 %copy-start.14 = (f32[4,256,256]{2,1,0:T(8,128)}, f32[4,256,256]{2,1,0:T(8,128)S(1)}, u32[]{:S(2)}) copy-start(f32[4,256,256]{2,1,0:T(8,128)S(1)} %fusion.268) | copy-start | bytes 3145732 | tf_op jit(solution)/shard_map/transpose(jvp())/while
  394.9 7.0 copy-start.55
  401.0 5.3 copy-start.46
  401.0 5.3 copy-start.56
  448.6 8.2 copy-start.54
  458.8 8.3 copy-start.65
  469.3 13.1 %copy-start.64 = (f32[6]{0:T(128)}, f32[6]{0:T(128)S(1)}, u32[]{:S(2)}) copy-start(f32[6]{0:T(128)S(1)} %get-tuple-element.1417) | copy-start | bytes 76 | tf_op jit(solution)/shard_map/transpose(jvp())/while
  469.3 29.7 %copy-start.39 = (pred[1,256,256,1]{2,1,3,0:T(8,128)(4,1)}, pred[1,256,256,1]{2,1,3,0:T(8,128)(4,1)S(1)}, u32[]{:S(2)}) copy-start(pred[1,256,256,1]{2,1,3,0:T(8,128)(4,1)S(1)} %iota_compare_fusion.5) | copy-start | bytes 196612 | tf_op jit(solution)/shard_map/transpose(jvp())/while
  497.0 14.7 %copy-start.44 = (f32[4,256,6]{1,2,0:T(8,128)}, f32[4,256,6]{1,2,0:T(8,128)S(1)}, u32[]{:S(2)}) copy-start(f32[4,256,6]{1,2,0:T(8,128)S(1)} %copy.515) | copy-start | bytes 73732 | tf_op jit(solution)/shard_map/transpose(jvp())/while
  499.0 12.6 %copy-start.14 = (f32[4,256,256]{2,1,0:T(8,128)}, f32[4,256,256]{2,1,0:T(8,128)S(1)}, u32[]{:S(2)}) copy-start(f32[4,256,256]{2,1,0:T(8,128)S(1)} %fusion.268) | copy-start | bytes 3145732 | tf_op jit(solution)/shard_map/transpose(jvp())/while
  511.7 7.0 copy-start.55
  517.7 5.3 copy-start.46
  517.7 5.3 copy-start.56
  565.3 8.3 copy-start.54
  575.5 8.3 copy-start.65
  597.5 227.3 %all-reduce.16.cloned.1.call-start = ((), (), s32[]{:S(2)}) async-start(), calls=%async_computation.10 | async-start | bytes 8650752 | tf_op jit(solution)/shard_map/psum | solution.py:299
  623.7 60.4 %copy-start.61 = (f32[4,3,640]{2,1,0:T(4,128)S(1)}, f32[4,3,640]{2,1,0:T(4,128)}, u32[]{:S(2)}) copy-start(f32[4,3,640]{2,1,0:T(4,128)} %copy-done.60) | copy-start | bytes 92164
  684.2 16.9 %copy-start.69 = (f32[640]{0:T(1024)S(1)}, f32[640]{0:T(1024)}, u32[]{:S(2)}) copy-start(f32[640]{0:T(1024)} %copy-done.68) | copy-start | bytes 7684
  684.2 16.9 %copy-start.71 = (f32[640]{0:T(1024)S(1)}, f32[640]{0:T(1024)}, u32[]{:S(2)}) copy-start(f32[640]{0:T(1024)} %copy-done.70) | copy-start | bytes 7684
  684.2 16.9 %copy-start.73 = (f32[640]{0:T(1024)S(1)}, f32[640]{0:T(1024)}, u32[]{:S(2)}) copy-start(f32[640]{0:T(1024)} %copy-done.72) | copy-start | bytes 7684
  684.2 16.9 %copy-start.75 = (f32[640]{0:T(1024)S(1)}, f32[640]{0:T(1024)}, u32[]{:S(2)}) copy-start(f32[640]{0:T(1024)} %copy-done.74) | copy-start | bytes 7684
  710.9 13.5 %copy-start.89 = (f32[6]{0:T(128)S(1)}, f32[6]{0:T(128)}, u32[]{:S(2)}) copy-start(f32[6]{0:T(128)} %param.33) | copy-start | bytes 76
  722.8 5.4 collective-permute-start.1
  740.6 197.4 %reduce-scatter.3.cloned.1.call-start = ((), (), s32[]{:S(2)}) async-start(), calls=%async_computation.4 | async-start | bytes 7864320 | tf_op jit(solution)/shard_map/reduce_scatter | solution.py:113
  746.5 305.3 %reduce-scatter.5.cloned.1.call-start = ((), (), s32[]{:S(2)}) async-start(), calls=%async_computation.7 | async-start | bytes 7864320 | tf_op jit(solution)/shard_map/reduce_scatter | solution.py:113
  760.9 12.0 %slice-start = ((f32[768,1030]{0,1:T(8,128)}), f32[768,6]{0,1:T(8,128)S(1)}, s32[]{:S(2)}) async-start(f32[768,1030]{0,1:T(8,128)} %copy-done.31), calls=%async_computation.11 | async-start | bytes 49152 | tf_op jit(solution)/shard_map/slice | solution.py:297
  760.9 12.0 %copy-start.93 = (f32[384]{0:T(512)S(1)}, f32[384]{0:T(512)}, u32[]{:S(2)}) copy-start(f32[384]{0:T(512)} %get-tuple-element.1040) | copy-start | bytes 4612
  824.8 5.6 copy-start.59
  826.2 111.8 %copy-start.32 = (bf16[1,512,768]{2,1,0:T(8,128)(2,1)S(1)}, bf16[1,512,768]{2,1,0:T(8,128)(2,1)}, u32[]{:S(2)}) copy-start(bf16[1,512,768]{2,1,0:T(8,128)(2,1)} %param.23) | copy-start | bytes 2359300
  828.2 223.6 %copy-start.35 = (bf16[1,512,768]{2,1,0:T(8,128)(2,1)S(1)}, bf16[1,512,768]{2,1,0:T(8,128)(2,1)}, u32[]{:S(2)}) copy-start(bf16[1,512,768]{2,1,0:T(8,128)(2,1)} %param.24) | copy-start | bytes 2359300
  (73 other events, 228.6 us)
Sparse Core Ops, SparseCore 0:
  9.6 25.7 all-gather.10
  36.9 65.1 all-gather.8
  156.9 29.8 all-gather.14
  188.2 63.4 all-gather.12
  314.3 27.3 all-gather.16
  597.6 86.4 all-reduce.13
  740.8 84.0 all-reduce.15
  827.2 110.8 reduce-scatter.2
  940.5 111.2 reduce-scatter.4
where the time goes:
time: 1070 us; the launch traced here: 1060 us
  waiting for transfers between devices  386 us (36%)
  other arithmetic  221 us (21%)
  local copies, waits for them, and re-layouts  178 us (17%)
  matrix products  162 us (15%)
  blocking collectives  86.1 us (8%)
  between operations  15.1 us (1%)
    reduce_scatter x2, waiting for transfers between devices, sum_rows(): lax.psum_scatter(term_fn(jnp.int32(0), rows * lax.axis_size('wb')), 'wb',...  218 us
    another operation x27, other arithmetic  110 us
    all_gather x2, waiting for transfers between devices, gather_rows(): return lax.all_gather(values, 'wb', axis=0, tiled=True)  65.2 us
    dot_general x6, matrix products, span_step(): jnp.einsum('gtsh,gshp->gthp', mix_weight, x_blk, precision=PRECISION_HIGH)  57.3 us
    psum x1, waiting for transfers between devices, head_total(): return lax.psum(values, 'wb')  55.5 us
    psum x3, blocking collectives, head_total(): return lax.psum(values, 'wb')  28.7 us
    psum x1, blocking collectives, body(): lax.psum((zx_part, bc_part, dt_part, kernel_grad, offset_grad, bias_part,...  27.2 us
    unnamed x146, local copies, waits for them, and re-layouts  24.1 us
  transfers between devices with their start and end apart: 11, of which 7 were waited for; matrix products, arithmetic and copies ran while one was open for 17% of the time, Pallas kernels for 0%

commit v1 on v0

v1 whole, which is shorter than its diff:
```python
import functools
import types

import jax
import jax.numpy as jnp
from jax import lax
from jax.experimental import pallas as pl
from jax.experimental.pallas import tpu as pltpu
from jax.sharding import PartitionSpec as P

F32, BF16 = jnp.float32, jnp.bfloat16
EPSILON = 1e-05
Q = 128
LANES = 128
HALO = 16
SLOTS = 16
TILE = 256
NT = (((1,), (1,)), ((), ()))


def dot(a, b):
    return jnp.dot(a, b, preferred_element_type=F32)


def dot_nt(a, b):
    return lax.dot_general(a, b, NT, preferred_element_type=F32)


def dot_exact(a, b):
    return jnp.dot(a, b, precision=lax.Precision.HIGHEST, preferred_element_type=F32)


def sigmoid(v):
    return 0.5 + 0.5 * jnp.tanh(0.5 * v)


def fold8(v):
    return v.reshape(v.shape[0] // 8, 8, v.shape[1]).sum(axis=0)


def rows_at(i, size=Q, base=0):
    return pl.ds(pl.multiple_of(i * size + base, 16), size)


def cols_at(i, size=LANES):
    return pl.ds(pl.multiple_of(i * size, LANES), size)


def head_spread(R, bands, head_dim):
    inner = R.ex.shape[1]
    per_band = inner // bands
    row = lax.broadcasted_iota(jnp.int32, (LANES, LANES), 0)

    @pl.loop(0, inner // LANES)
    def _(c):
        lane = lax.broadcasted_iota(jnp.int32, (LANES, LANES), 1) + c * LANES
        hit = jnp.zeros((LANES, LANES), jnp.bool_)
        for band in range(bands):
            first = lane - band * per_band
            inside = (first >= 0) & (first < per_band)
            head = lax.shift_right_arithmetic(first, head_dim.bit_length() - 1)
            hit = hit | (inside & (row == band * SLOTS + head))
        R.ex[:, cols_at(c)] = jnp.where(hit, 1.0, 0.0).astype(BF16)


def norm_rows(R):
    gain = R.gain[...]

    def normed(rows):
        inv = lax.rsqrt(jnp.mean(rows * rows, axis=-1, keepdims=True) + EPSILON)
        return (rows * inv * gain).astype(BF16), inv

    @pl.loop(0, R.x.shape[0] // Q)
    def _(i):
        value, inv = normed(R.x[rows_at(i), :].astype(F32))
        R.xn[rows_at(i, base=HALO), :] = value
        R.inv_rms[rows_at(i), :] = inv
        R.xnT[:, cols_at(i)] = value.T
        R.gT[:, cols_at(i)] = R.g[rows_at(i), :].T


def norm_halo(R):
    rows = R.x_halo[...].astype(F32)
    inv = lax.rsqrt(jnp.mean(rows * rows, axis=-1, keepdims=True) + EPSILON)
    R.xn[0:HALO, :] = (rows * inv * R.gain[...]).astype(BF16)


def project_x(R):
    inner = R.wx.shape[1]

    @pl.loop(0, inner // TILE)
    def _(j):
        R.ci[:, cols_at(j, TILE)] = dot(R.xn[...], R.wx[:, cols_at(j, TILE)])

    R.ci[:, inner:] = dot(R.xn[...], R.wbc[...])


def project_z(R):
    @pl.loop(0, R.wz.shape[1] // TILE)
    def _(j):
        R.z[:, cols_at(j, TILE)] = dot(R.xn[HALO:, :], R.wz[:, cols_at(j, TILE)])


def convolve(R, taps):
    length = R.x.shape[0]
    inner = R.wx.shape[1]

    def tile(cols, put):
        for i in range(length // Q):
            pre = R.par[4:5, cols]
            for k in range(taps):
                first = HALO - (taps - 1) + k + i * Q
                pre = pre + R.par[k : k + 1, cols] * R.ci[pl.ds(first, Q), cols]
            sig = sigmoid(pre)
            act = pre * sig
            put(pl.ds(i * Q, Q), act)
            R.slope[pl.ds(i * Q, Q), cols] = (sig + act * (1.0 - sig)).astype(BF16)

    @pl.loop(0, inner // LANES)
    def _(c):
        def put(rows, act):
            R.xh[rows, cols_at(c)] = act.astype(BF16)

        tile(cols_at(c), put)

    def put_b(rows, act):
        R.bm[rows, :] = act.astype(BF16)

    def put_c(rows, act):
        R.cm[rows, :] = act.astype(BF16)

    tile(pl.ds(inner, LANES), put_b)
    tile(pl.ds(inner + LANES, LANES), put_c)


def lower_ones(strict=False):
    row = lax.broadcasted_iota(jnp.int32, (Q, Q), 0)
    col = lax.broadcasted_iota(jnp.int32, (Q, Q), 1)
    return jnp.where(row > col if strict else row >= col, 1.0, 0.0).astype(F32)


def step_sizes(R):
    R.rate[...] = -jnp.exp(R.par[8:9, 0:LANES])
    bias, rate = R.par[7:8, 0:LANES], R.rate[...]
    ones = lower_ones()
    chunks = R.x.shape[0] // Q
    R.ends[...] = jnp.zeros_like(R.ends)
    for i in range(chunks):
        rows = pl.ds(i * Q, Q)
        v = dot_nt(R.xn[pl.ds(HALO + i * Q, Q), :], R.wdt[...]) + bias
        dt = jnp.maximum(v, 0.0) + jnp.log1p(jnp.exp(-jnp.abs(v)))
        R.dt[rows, :] = dt
        R.dt_sig[rows, :] = jax.nn.sigmoid(v)
        logs = dot_exact(ones, dt * rate)
        R.logs[rows, :] = logs
        R.logsT[:, rows] = logs.T
        last = logs[Q - 1 : Q, :]
        R.ends[i : i + 1, :] = last
        R.dtx[rows, :] = dot(dt.astype(BF16), R.ex[...]).astype(BF16)
        R.expx[rows, :] = dot(jnp.exp(logs).astype(BF16), R.ex[...]).astype(BF16)
        R.tailx[rows, :] = dot(jnp.exp(last - logs).astype(BF16), R.ex[...]).astype(BF16)
    decay = jnp.exp(R.ends[...])
    high = decay.astype(BF16)
    low = (decay - high.astype(F32)).astype(BF16)
    R.decx[...] = dot(high, R.ex[...]) + dot(low, R.ex[...])


def local_states(R):
    chunks = R.x.shape[0] // Q

    @pl.loop(0, chunks)
    def _(i):
        rows = rows_at(i)
        weighted = R.xh[rows, :].astype(F32) * R.dtx[rows, :].astype(F32)
        R.xt[rows, :] = weighted.astype(BF16)
        R.sl[i] = dot(
            R.bm[rows, :].T, (weighted * R.tailx[rows, :].astype(F32)).astype(BF16)
        ).astype(BF16)

    total = R.sl[0].astype(F32)
    for i in range(1, chunks):
        total = total * R.decx[i : i + 1, :] + R.sl[i].astype(F32)
    R.piece[...] = total
    decay = R.decx[0:1, :]
    for i in range(1, chunks):
        decay = decay * R.decx[i : i + 1, :]
    R.piece_decay[...] = decay


def lane_half(value, half):
    lane = lax.broadcasted_iota(jnp.int32, value.shape, 1)
    keep = lane < LANES // 2 if half == 0 else lane >= LANES // 2
    return jnp.where(keep, value, jnp.zeros_like(value))


def slot_of(head, per_band):
    return head // per_band * SLOTS + head % per_band


def inside_forward(R, per_band):
    heads = R.wx.shape[1] // (LANES // 2)

    @pl.loop(0, R.x.shape[0] // Q)
    def _(i):
        rows = rows_at(i)
        row = lax.broadcasted_iota(jnp.int32, (Q, Q), 0)
        col = lax.broadcasted_iota(jnp.int32, (Q, Q), 1)
        causal = row >= col
        inner_prod = dot_nt(R.cm[rows, :], R.bm[rows, :])
        logs = R.logs[rows, :]
        for pair in range(heads // 2):
            cols = pl.ds(pair * LANES, LANES)
            xt = R.xt[rows, cols]
            total = None
            for half in range(2):
                slot = slot_of(2 * pair + half, per_band)
                gap = logs[:, slot : slot + 1] - R.logsT[slot : slot + 1, rows]
                decay = jnp.exp(jnp.where(causal, gap, -1e30))
                part = dot((inner_prod * decay).astype(BF16), lane_half(xt, half))
                total = part if total is None else total + part
            R.y[rows, cols] = total


def carried_forward(R):
    chunks = R.x.shape[0] // Q
    R.state[...] = R.from_before[...].astype(F32)

    @pl.loop(0, chunks)
    def _(i):
        rows = rows_at(i)
        state = R.state[...]
        R.s_in[i] = state.astype(BF16)
        carried = dot(R.cm[rows, :], R.s_in[i]) * R.expx[rows, :].astype(F32)
        R.yi[rows, :] = carried.astype(BF16)
        R.y[rows, :] += carried
        R.state[...] = state * R.decx[pl.ds(i, 1), :] + R.sl[i].astype(F32)


def hidden_grad(R):
    @pl.loop(0, R.x.shape[0] // Q)
    def _(i):
        R.dh[rows_at(i), :] = dot(R.g[rows_at(i), :], R.wo[...]).astype(BF16)


def gate(R):
    inner = R.wx.shape[1]
    R.gain_acc[...] = jnp.zeros_like(R.gain_acc)
    R.skip_acc[...] = jnp.zeros_like(R.skip_acc)

    @pl.loop(0, R.x.shape[0] // Q)
    def _(i):
        rows = rows_at(i)

        def first(c, sums):
            cols = cols_at(c)
            y = R.y[rows, cols] + R.par[6:7, cols] * R.xh[rows, cols].astype(F32)
            R.y[rows, cols] = y
            z = R.z[rows, cols]
            gated = (y * (z * sigmoid(z))).astype(BF16)
            R.gated[rows, cols] = gated
            gated = gated.astype(F32)
            return (
                sums[0] + gated * gated,
                sums[1] + gated * (R.dh[rows, cols].astype(F32) * R.par[5:6, cols]),
            )

        zero = jnp.zeros((Q, LANES), F32)
        squares, cross = lax.fori_loop(0, inner // LANES, first, (zero, zero))
        inv = lax.rsqrt(jnp.sum(squares, axis=-1, keepdims=True) / inner + EPSILON)
        cross = jnp.sum(cross, axis=-1, keepdims=True) * (inv * inv * inv / inner)
        inv = jnp.broadcast_to(inv, (Q, LANES))
        cross = jnp.broadcast_to(cross, (Q, LANES))

        @pl.loop(0, inner // LANES)
        def _(c):
            cols = cols_at(c)
            gated = R.gated[rows, cols].astype(F32)
            dh = R.dh[rows, cols].astype(F32)
            gain = R.par[5:6, cols]
            scaled = gated * inv
            R.hidden[rows, cols] = (scaled * gain).astype(BF16)
            R.gain_acc[:, cols] += fold8(dh * scaled)
            d_gated = dh * gain * inv - gated * cross
            z = R.z[rows, cols]
            sig = sigmoid(z)
            lin = z * sig
            dy = d_gated * lin
            R.dz[rows, cols] = (d_gated * R.y[rows, cols] * (sig + lin * (1.0 - sig))).astype(BF16)
            R.dy[rows, cols] = dy.astype(BF16)
            R.dyl[rows, cols] = (dy * R.expx[rows, cols].astype(F32)).astype(BF16)
            R.skip_acc[:, cols] += fold8(dy * R.xh[rows, cols].astype(F32))


def branch_out(R):
    @pl.loop(0, R.x.shape[0] // Q)
    def _(i):
        rows = rows_at(i)
        R.layer_out[rows, :] = (
            R.x[rows, :].astype(F32) + dot_nt(R.hidden[rows, :], R.wo[...])
        ).astype(BF16)


def grad_tiles(left, right, out):
    @pl.loop(0, right.shape[1] // TILE)
    def _(j):
        cols = cols_at(j, TILE)
        out[:, cols] = dot(left[...], right[:, cols]).astype(out.dtype)


def local_adjoints(R):
    chunks = R.x.shape[0] // Q

    @pl.loop(0, chunks)
    def _(i):
        rows = rows_at(i)
        R.dl[i] = dot(R.cm[rows, :].T, R.dyl[rows, :]).astype(BF16)

    total = R.dl[chunks - 1].astype(F32)
    for i in range(chunks - 2, -1, -1):
        total = total * R.decx[i : i + 1, :] + R.dl[i].astype(F32)
    R.piece[...] = total


def inside_backward(R, per_band):
    heads = R.wx.shape[1] // (LANES // 2)

    @pl.loop(0, R.x.shape[0] // Q)
    def _(i):
        rows = rows_at(i)
        row = lax.broadcasted_iota(jnp.int32, (Q, Q), 0)
        col = lax.broadcasted_iota(jnp.int32, (Q, Q), 1)
        causal = row <= col
        prod = dot_nt(R.bm[rows, :], R.cm[rows, :])
        logs = R.logs[rows, :]
        d_prod = jnp.zeros((Q, Q), F32)
        columns = jnp.zeros((Q, LANES), F32)
        R.pulls[...] = jnp.zeros_like(R.pulls)
        for pair in range(heads // 2):
            cols = pl.ds(pair * LANES, LANES)
            xt = R.xt[rows, cols]
            dy = R.dy[rows, cols]
            total = None
            for half in range(2):
                slot = slot_of(2 * pair + half, per_band)
                gap = R.logsT[slot : slot + 1, rows] - logs[:, slot : slot + 1]
                decay = jnp.exp(jnp.where(causal, gap, -1e30))
                dy_half = lane_half(dy, half)
                mix = prod * decay
                part = dot(mix.astype(BF16), dy_half)
                total = part if total is None else total + part
                d_mix = dot_nt(xt, dy_half)
                d_prod = d_prod + decay * d_mix
                pull = mix * d_mix
                R.pulls[slot : slot + 1, :] = jnp.sum(pull, axis=0, keepdims=True)
                columns = jnp.where(col == slot, jnp.sum(pull, axis=1, keepdims=True), columns)
            R.u[rows, cols] = total
        R.d_log[rows, :] = R.pulls[...].T - columns
        d_prod = d_prod.astype(BF16)
        R.db[rows, :] = dot(d_prod, R.cm[rows, :])
        R.dc[rows, :] = dot(d_prod.T, R.bm[rows, :])


def carried_backward(R):
    chunks = R.x.shape[0] // Q
    R.state[...] = R.from_after[...].astype(F32)
    later = lower_ones().T
    before = lower_ones(strict=True)
    R.rate_acc[...] = jnp.zeros_like(R.rate_acc)
    R.bias_acc[...] = jnp.zeros_like(R.bias_acc)

    @pl.loop(0, chunks)
    def _(k):
        i = chunks - 1 - k
        rows = rows_at(i)
        grad = R.state[...]
        grad_low = grad.astype(BF16)
        tail = R.tailx[rows, :].astype(F32)
        xt = R.xt[rows, :].astype(F32)
        pulled = dot(R.bm[rows, :], grad_low) * tail
        R.u[rows, :] += pulled
        tails = dot_nt((xt * pulled).astype(BF16), R.ex[...])
        R.db[rows, :] += dot_nt((xt * tail).astype(BF16), grad_low)
        R.dc[rows, :] += dot_nt(R.dyl[rows, :], R.s_in[i])
        inter = dot_nt(
            (R.dy[rows, :].astype(F32) * R.yi[rows, :].astype(F32)).astype(BF16), R.ex[...]
        )
        decay = R.decx[pl.ds(i, 1), :]
        kept = jnp.sum(grad * R.s_in[i].astype(F32), axis=0, keepdims=True) * decay
        kept = dot_nt(jnp.broadcast_to(kept, (8, kept.shape[1])).astype(BF16), R.ex[...])[0:1, :]
        R.state[...] = grad * decay + R.dl[i].astype(F32)
        d_decay = dot_exact(later, R.d_log[rows, :] + inter) + dot_exact(before, tails) + kept
        direct = dot_nt((R.xh[rows, :].astype(F32) * R.u[rows, :]).astype(BF16), R.ex[...])
        d_raw = (direct + R.rate[...] * d_decay) * R.dt_sig[rows, :]
        R.rate_acc[...] += fold8(R.dt[rows, :] * d_decay)
        R.bias_acc[...] += fold8(d_raw)
        R.d_raw[rows, :] = d_raw.astype(BF16)


def before_conv(R):
    inner = R.wx.shape[1]

    @pl.loop(0, inner // LANES)
    def _(c):
        cols = cols_at(c)
        skip = R.par[6:7, cols]

        @pl.loop(0, R.x.shape[0] // Q)
        def _(i):
            rows = rows_at(i)
            dx = R.dtx[rows, cols].astype(F32) * R.u[rows, cols] + skip * R.dy[rows, cols].astype(F32)
            R.dpre[rows, cols] = dx * R.slope[rows, cols].astype(F32)

    length = R.x.shape[0]
    R.dpre[0:length, inner : inner + LANES] = R.db[...] * R.slope[:, inner : inner + LANES].astype(F32)
    R.dpre[0:length, inner + LANES :] = R.dc[...] * R.slope[:, inner + LANES :].astype(F32)


def conv_backward(R, taps):
    length = R.x.shape[0]
    width = R.ci.shape[1]

    @pl.loop(0, width // LANES)
    def _(c):
        cols = cols_at(c)
        sums = [jnp.zeros((8, LANES), F32) for _ in range(taps + 1)]
        for i in range(length // Q):
            base = i * Q
            here = R.dpre[pl.ds(base, Q), cols]
            sums[taps] = sums[taps] + fold8(here)
            d_conv = None
            for k in range(taps):
                sums[k] = sums[k] + fold8(here * R.ci[pl.ds(HALO - (taps - 1) + k + base, Q), cols])
                term = R.par[k : k + 1, cols] * R.dpre[pl.ds(base + taps - 1 - k, Q), cols]
                d_conv = term if d_conv is None else d_conv + term
            R.dconv[pl.ds(base, Q), cols] = d_conv.astype(BF16)
        for k in range(taps + 1):
            R.vec[k : k + 1, cols] = jnp.sum(sums[k], axis=0, keepdims=True)


def input_side(R):
    gain = R.gain[...]
    inner = R.wx.shape[1]
    R.norm_acc[...] = jnp.zeros_like(R.norm_acc)

    @pl.loop(0, R.x.shape[0] // Q)
    def _(i):
        rows = rows_at(i)
        d_normed = (
            dot_nt(R.dz[rows, :], R.wz[...])
            + dot_nt(R.dconv[rows, 0:inner], R.wx[...])
            + dot_nt(R.dconv[rows, inner:], R.wbc[...])
            + dot(R.d_raw[rows, :], R.wdt[...])
        )
        x = R.x[rows, :].astype(F32)
        inv = R.inv_rms[rows, :]
        R.norm_acc[...] += fold8(d_normed * x * inv)
        d_scaled = d_normed * gain
        middle = jnp.mean(d_scaled * x, axis=-1, keepdims=True)
        R.input_grad[rows, :] = (
            R.g[rows, :].astype(F32) + inv * d_scaled - x * (inv * inv * inv * middle)
        )


def small_sums(R):
    inner = R.wx.shape[1]
    width = R.gain.shape[1]
    R.vec[5:16, :] = jnp.zeros((11, R.vec.shape[1]), F32)
    R.vec[5:6, 0:inner] = jnp.sum(R.gain_acc[...], axis=0, keepdims=True)
    R.vec[6:7, 0:width] = jnp.sum(R.norm_acc[...], axis=0, keepdims=True)
    R.vec[7:8, 0:LANES] = jnp.sum(R.bias_acc[...], axis=0, keepdims=True)
    R.vec[8:9, 0:LANES] = jnp.sum(R.rate_acc[...], axis=0, keepdims=True) * R.rate[...]
    skip = R.skip_acc[...]
    high = skip.astype(BF16)
    low = (skip - high.astype(F32)).astype(BF16)
    R.vec[9:10, 0:LANES] = jnp.sum(
        dot_nt(high, R.ex[...]) + dot_nt(low, R.ex[...]), axis=0, keepdims=True
    )


def neighbour(R, at):
    return {"seq": at}


def send(R, src, dst, index, at):
    return pltpu.make_async_remote_copy(
        src_ref=src,
        dst_ref=dst,
        send_sem=R.send_sem.at[index],
        recv_sem=R.recv_sem.at[index],
        device_id=neighbour(R, at),
        device_id_type=pl.DeviceIdType.MESH,
    )


PARTS = 3


def chain(R, first_sem, landing, place, count, step):
    has_from = place > 0 if step > 0 else place < count - 1
    has_to = place < count - 1 if step > 0 else place > 0
    width = R.piece.shape[1] // PARTS
    for part in range(PARTS):
        cols = pl.ds(part * width, width)
        copy = send(R, R.outgoing.at[:, cols], landing.at[:, cols], first_sem + part, place + step)

        @pl.when(has_from)
        def _():
            copy.wait_recv()

        @pl.when(has_to)
        def _():
            incoming = landing[:, cols].astype(F32)
            R.outgoing[:, cols] = (
                R.piece[:, cols] + R.piece_decay[:, cols] * incoming
            ).astype(BF16)
            copy.start()


def chain_sent(R, first_sem, landing, place, count, step):
    has_to = place < count - 1 if step > 0 else place > 0
    width = R.piece.shape[1] // PARTS

    @pl.when(has_to)
    def _():
        for part in range(PARTS):
            cols = pl.ds(part * width, width)
            send(R, R.outgoing.at[:, cols], landing.at[:, cols], first_sem + part, place + step).wait_send()


X_SEM, FWD_SEM, BWD_SEM, PRE_SEM, SEMS = 0, 1, 1 + PARTS, 1 + 2 * PARTS, 2 + 2 * PARTS


def layer(names, bands, head_dim, taps, *refs):
    R = types.SimpleNamespace(**dict(zip(names, refs)))
    R.dl, R.u, R.dyl, R.state = R.sl, R.z, R.gated, R.piece
    R.y = R.dpre.at[0 : R.x.shape[0], 0 : R.wx.shape[1]]
    count = lax.axis_size("seq")
    place = lax.axis_index("seq")
    per_band = R.wx.shape[1] // head_dim // bands
    length = R.x.shape[0]
    first, last = place == 0, place == count - 1

    barrier = pltpu.get_barrier_semaphore()

    @pl.when(jnp.logical_not(last))
    def _():
        pl.semaphore_signal(barrier, 1, device_id=neighbour(R, place + 1), device_id_type=pl.DeviceIdType.MESH)

    @pl.when(jnp.logical_not(first))
    def _():
        pl.semaphore_signal(barrier, 1, device_id=neighbour(R, place - 1), device_id_type=pl.DeviceIdType.MESH)

    pl.semaphore_wait(barrier, jnp.where(first | last, 1, 2))

    x_copy = send(R, R.x.at[pl.ds(length - HALO, HALO), :], R.x_halo, X_SEM, place + 1)

    @pl.when(jnp.logical_not(last))
    def _():
        x_copy.start()

    @pl.when(first)
    def _():
        R.x_halo[...] = jnp.zeros_like(R.x_halo)
        R.from_before[...] = jnp.zeros_like(R.from_before)

    @pl.when(last)
    def _():
        R.from_after[...] = jnp.zeros_like(R.from_after)
        R.dpre_halo[...] = jnp.zeros_like(R.dpre_halo)

    head_spread(R, bands, head_dim)
    norm_rows(R)

    @pl.when(jnp.logical_not(first))
    def _():
        x_copy.wait_recv()

    norm_halo(R)
    project_x(R)
    convolve(R, taps)
    step_sizes(R)
    local_states(R)
    early = place < count // 2

    @pl.when(early)
    def _():
        chain(R, FWD_SEM, R.from_before, place, count, 1)

    project_z(R)
    hidden_grad(R)
    inside_forward(R, per_band)

    @pl.when(jnp.logical_not(early))
    def _():
        chain(R, FWD_SEM, R.from_before, place, count, 1)

    carried_forward(R)
    chain_sent(R, FWD_SEM, R.from_before, place, count, 1)
    gate(R)
    local_adjoints(R)

    @pl.when(jnp.logical_not(early))
    def _():
        chain(R, BWD_SEM, R.from_after, place, count, -1)

    branch_out(R)
    grad_tiles(R.gT, R.hidden, R.go)
    grad_tiles(R.xnT, R.dz, R.gz)
    inside_backward(R, per_band)

    @pl.when(early)
    def _():
        chain(R, BWD_SEM, R.from_after, place, count, -1)

    carried_backward(R)
    chain_sent(R, BWD_SEM, R.from_after, place, count, -1)
    before_conv(R)
    R.dpre_out[...] = R.dpre[0:HALO, :].astype(BF16)
    pre_copy = send(R, R.dpre_out, R.dpre_halo, PRE_SEM, place - 1)

    @pl.when(jnp.logical_not(first))
    def _():
        pre_copy.start()

    @pl.when(jnp.logical_not(last))
    def _():
        pre_copy.wait_recv()

    R.dpre[pl.ds(length, HALO), :] = R.dpre_halo[...].astype(F32)
    conv_backward(R, taps)
    grad_tiles(R.xnT, R.dconv.at[:, 0 : R.wx.shape[1]], R.gx)
    R.gbc[...] = dot(R.xnT[...], R.dconv[:, R.wx.shape[1] :]).astype(R.gbc.dtype)
    R.gdt[...] = dot(R.d_raw[...].T, R.xn[HALO:, :]).astype(R.gdt.dtype)
    input_side(R)
    small_sums(R)

    @pl.when(jnp.logical_not(last))
    def _():
        x_copy.wait_send()

    @pl.when(jnp.logical_not(first))
    def _():
        pre_copy.wait_send()


def run_layer(x, g, gain, wz, wx, wbc, wdt, wo, par, bands, head_dim, taps):
    length, width = x.shape
    inner = wz.shape[1]
    conv = inner + wbc.shape[1]
    chunks = length // Q
    ins = dict(x=x, g=g, gain=gain, wz=wz, wx=wx, wbc=wbc, wdt=wdt, wo=wo, par=par)
    outs = dict(
        layer_out=((length, width), BF16),
        input_grad=((length, width), F32),
        gz=((width, inner), BF16),
        gx=((width, inner), BF16),
        go=((width, inner), BF16),
        gbc=((width, wbc.shape[1]), BF16),
        gdt=((LANES, width), F32),
        vec=((16, conv), F32),
    )
    scratch = dict(
        ex=((LANES, inner), BF16),
        xn=((HALO + length, width), BF16),
        xnT=((width, length), BF16),
        gT=((width, length), BF16),
        inv_rms=((length, 1), F32),
        x_halo=((HALO, width), BF16),
        ci=((HALO + length, conv), F32),
        z=((length, inner), F32),
        xh=((length, inner), BF16),
        xt=((length, inner), BF16),
        bm=((length, LANES), BF16),
        cm=((length, LANES), BF16),
        slope=((length, conv), BF16),
        rate=((1, LANES), F32),
        dt=((length, LANES), F32),
        dt_sig=((length, LANES), F32),
        logs=((length, LANES), F32),
        logsT=((LANES, length), F32),
        ends=((8, LANES), F32),
        decx=((8, inner), F32),
        dtx=((length, inner), BF16),
        expx=((length, inner), BF16),
        tailx=((length, inner), BF16),
        sl=((chunks, LANES, inner), BF16),
        s_in=((chunks, LANES, inner), BF16),
        piece=((LANES, inner), F32),
        piece_decay=((1, inner), F32),
        outgoing=((LANES, inner), BF16),
        from_before=((LANES, inner), BF16),
        from_after=((LANES, inner), BF16),
        yi=((length, inner), BF16),
        dh=((length, inner), BF16),
        gated=((length, inner), BF16),
        hidden=((length, inner), BF16),
        dz=((length, inner), BF16),
        dy=((length, inner), BF16),
        gain_acc=((8, inner), F32),
        skip_acc=((8, inner), F32),
        norm_acc=((8, width), F32),
        rate_acc=((8, LANES), F32),
        bias_acc=((8, LANES), F32),
        pulls=((LANES, Q), F32),
        d_log=((length, LANES), F32),
        db=((length, LANES), F32),
        dc=((length, LANES), F32),
        d_raw=((length, LANES), BF16),
        dpre=((length + HALO, conv), F32),
        dpre_out=((HALO, conv), BF16),
        dpre_halo=((HALO, conv), BF16),
        dconv=((length, conv), BF16),
    )
    names = (*ins, *outs, *scratch, "send_sem", "recv_sem")
    return pl.pallas_call(
        functools.partial(layer, names, bands, head_dim, taps),
        out_shape=[jax.ShapeDtypeStruct(*v) for v in outs.values()],
        in_specs=[pl.BlockSpec(memory_space=pltpu.VMEM)] * len(ins),
        out_specs=[pl.BlockSpec(memory_space=pltpu.VMEM)] * len(outs),
        scratch_shapes=[pltpu.VMEM(*v) for v in scratch.values()]
        + [pltpu.SemaphoreType.DMA((SEMS,)), pltpu.SemaphoreType.DMA((SEMS,))],
        compiler_params=pltpu.CompilerParams(
            collective_id=0, has_side_effects=True, vmem_limit_bytes=VMEM_BYTES
        ),
    )(*ins.values())


VMEM_BYTES = 64 * 2**20 - 2**18


def body(residual, cotangent, norm_gain, w_zx, w_bc, w_dt, x_kernel, x_offset, bc_kernel, bc_offset, dt_bias, a_log, d_skip, gate_gain, w_out):
    pieces, length, width = residual.shape
    bands = lax.axis_size("wb")
    heads_own, inner_own, state = w_dt.shape[1], w_zx.shape[2], w_bc.shape[2]
    heads, inner, conv = heads_own * bands, inner_own * bands, inner_own * bands + 2 * state
    head_dim = inner_own // heads_own
    taps = x_kernel.shape[0]
    groups = LANES // SLOTS
    groups = min(groups, 4)
    wzx = lax.all_gather(lax.all_gather(w_zx, "wa", axis=0, tiled=True), "wb", axis=2, tiled=True)
    wbc = lax.all_gather(w_bc, "wa", axis=0, tiled=True).reshape(width, 2 * state)
    wdt = lax.all_gather(lax.all_gather(w_dt, "wa", axis=0, tiled=True), "wb", axis=1, tiled=True)
    wo = lax.all_gather(lax.all_gather(w_out, "wa", axis=0, tiled=True), "wb", axis=1, tiled=True)
    per = heads // groups

    def slots(rows):
        rows = rows.reshape(groups, per, -1)
        rows = jnp.pad(rows, ((0, 0), (0, SLOTS - per), (0, 0))).reshape(groups * SLOTS, -1)
        return jnp.pad(rows, ((0, LANES - groups * SLOTS), (0, 0)))

    def unslots(rows):
        return rows[: groups * SLOTS].reshape(groups, SLOTS, -1)[:, :per].reshape(heads, -1)

    own = jnp.concatenate(
        [
            x_kernel.astype(F32),
            x_offset.astype(F32)[None],
            gate_gain.astype(F32)[None],
            jnp.repeat(d_skip, head_dim)[None],
        ],
        axis=0,
    )
    par_x = lax.all_gather(own, "wb", axis=1, tiled=True)
    small = lax.all_gather(jnp.stack([dt_bias, a_log]), "wb", axis=1, tiled=True)
    par_bc = jnp.concatenate(
        [bc_kernel.reshape(taps, 2 * state).astype(F32), bc_offset.reshape(1, 2 * state).astype(F32), jnp.zeros((2, 2 * state), F32)], axis=0
    )
    par = jnp.concatenate([par_x, par_bc], axis=1)
    rows = jnp.pad(slots(small.T).T, ((0, 0), (0, conv - LANES)))
    par = jnp.concatenate([par, rows, jnp.zeros((7, conv), F32)], axis=0)
    layer_out, input_grad, gz, gx, go, gbc, gdt, vec = run_layer(
        residual.reshape(length, width),
        cotangent.reshape(length, width),
        norm_gain.astype(F32)[None],
        wzx[:, 0],
        wzx[:, 1],
        wbc,
        slots(wdt.T),
        wo,
        par,
        groups,
        head_dim,
        taps,
    )

    def share(grad, columns=True):
        grad = grad.astype(F32)
        grad = lax.psum_scatter(grad, "wa", scatter_dimension=0, tiled=True)
        if columns:
            grad = lax.psum_scatter(grad, "wb", scatter_dimension=grad.ndim - 1, tiled=True)
        else:
            grad = lax.psum(grad, "wb")
        return lax.psum(grad, "seq")

    zx_grad = share(jnp.stack([gz, gx], axis=1))
    bc_grad = share(gbc, False).reshape(-1, 2, state)
    dt_grad = share(unslots(gdt).T)
    out_grad = share(go)
    vec = lax.psum(vec, ("seq", "wa", "wb"))
    mine = lax.axis_index("wb")
    wide = lax.dynamic_slice_in_dim(vec[:, :inner], mine * inner_own, inner_own, 1)
    heads_vec = unslots(vec[7:10, :LANES].T)
    heads_vec = lax.dynamic_slice_in_dim(heads_vec, mine * heads_own, heads_own, 0)
    return (
        layer_out.reshape(residual.shape),
        input_grad.reshape(residual.shape),
        vec[6, :width],
        zx_grad,
        bc_grad,
        dt_grad,
        wide[0:taps],
        wide[4],
        vec[0:taps, inner:].reshape(taps, 2, state),
        vec[4, inner:].reshape(2, state),
        heads_vec[:, 0],
        heads_vec[:, 1],
        heads_vec[:, 2],
        wide[5],
        out_grad,
    )


def solution(mesh):
    batch = P(("wa", "wb"), "seq", None)
    ins = (
        batch, batch, P(), P("wa", None, "wb"), P("wa", None, None), P("wa", "wb"), P(None, "wb"), P("wb"), P(), P(),
        P("wb"), P("wb"), P("wb"), P("wb"), P("wa", "wb"),
    )
    outs = (
        batch, batch, P(), P("wa", None, "wb"), P("wa", None, None), P("wa", "wb"), P(None, "wb"), P("wb"), P(), P(),
        P("wb"), P("wb"), P("wb"), P("wb"), P("wa", "wb"),
    )
    return jax.shard_map(body, mesh=mesh, in_specs=ins, out_specs=outs, check_vma=False)
```

time: 1070 us -> 848 us (0.79)
  waiting for transfers between devices: 386 us -> 616 us
  other arithmetic: 221 us -> 13.1 us
  matrix products: 162 us -> 0 us
  local copies, waits for them, and re-layouts: 178 us -> 28.8 us
  Pallas kernels: 0 us -> 84.2 us
    dot_general x36 -> x0, matrix products: 162 us -> none  [the longest x6 57.3 us: span_step(): jnp.einsum('gtsh,gshp->gthp', mix_weight, x_blk, precision=PRECISION_HIGH)]
    another operation x28 -> x0, other arithmetic: 113 us -> none
    psum x2 -> x3, waiting for transfers between devices: 77.3 us -> 189 us  [the longest x1 126 us: body(): vec = lax.psum(vec, ('seq', 'wa', 'wb'))]
    reduce_scatter x2 -> x6, waiting for transfers between devices: 218 us -> 324 us  [the longest x4 189 us: share(): grad = lax.psum_scatter(grad, 'wa', scatter_dimension=0, tiled=True)]
    pallas_call x0 -> x1, Pallas kernels: none -> 84.2 us  [run_layer(): pl.pallas_call(functools.partial(layer, names, bands, head_dim, taps), ou...]
    psum x4 -> x1, blocking collectives: 56 us -> 11.6 us  [share(): return lax.psum(grad, 'seq')]
    reduce_sum x10 -> x0, other arithmetic: 41 us -> none  [the longest x1 16.8 us: causal_conv(): kernel[tap_index] * padded[:, tap_index:tap_index + steps_out]]
    another operation x66 -> x1, local copies, waits for them, and re-layouts: 40.4 us -> 0.08 us  [body(): jnp.repeat(d_skip, head_dim)[None]]
  transfers between devices with their start and end apart: 11 -> 12, of which waited for: 7 -> 12; matrix products, arithmetic and copies ran while one was open for 17% -> 3% of each run, Pallas kernels for 0% -> 0%
where the time goes in v1:
time: 848 us
  waiting for transfers between devices  616 us (73%)
  blocking collectives  90.2 us (11%)
  Pallas kernels  84.2 us (10%)
  local copies, waits for them, and re-layouts  28.8 us (3%)
  between operations  15.2 us (2%)
  other arithmetic  13.1 us (2%)
    reduce_scatter x4, waiting for transfers between devices, share(): grad = lax.psum_scatter(grad, 'wa', scatter_dimension=0, tiled=True)  189 us
    reduce_scatter x2, waiting for transfers between devices, share(): lax.psum_scatter(grad, 'wb', scatter_dimension=grad.ndim - 1, tiled=True)  135 us
    psum x1, waiting for transfers between devices, body(): vec = lax.psum(vec, ('seq', 'wa', 'wb'))  126 us
    pallas_call x1, Pallas kernels, run_layer(): pl.pallas_call(functools.partial(layer, names, bands, head_dim, taps), ou...  84.2 us
    all_gather x1, waiting for transfers between devices, body(): lax.all_gather(lax.all_gather(w_out, 'wa', axis=0, tiled=True), 'wb', axi...  45.8 us
    psum x1, waiting for transfers between devices, share(): grad = lax.psum(grad, 'wb')  37.7 us
    all_gather x1, waiting for transfers between devices, body(): lax.all_gather(lax.all_gather(w_zx, 'wa', axis=0, tiled=True), 'wb', axis...  30.2 us
    all_gather x1, waiting for transfers between devices, body(): lax.all_gather(w_zx, 'wa', axis=0, tiled=True)  26.3 us
  transfers between devices with their start and end apart: 12, of which 12 were waited for; matrix products, arithmetic and copies ran while one was open for 3% of the time, Pallas kernels for 0%

profile of v1, /device:TPU:0, one launch (start us, length us, event | category | flops | bytes accessed | tf_op | source)
XLA Modules:
  0.0 847.6 jit_solution(4125134279352219824)
XLA Ops:
  7.4 2.1 copy.36
  9.5 0.0 all-gather.8.cloned.1.call-start
  9.5 26.3 %all-gather.6.cloned.1.call-done = bf16[768,2,384]{2,0,1:T(8,128)(2,1)} async-done(((bf16[384,2,384]{2,0,1:T(8,128)(2,1)}), bf16[768,2,384]{2,0,1:T(8,128)(2,1)}) %all-gather.6.cloned.1.call-update) | async-done | bytes 1179664 | tf_op jit(solution)/shard_map/all_gather | solution.py:740
  35.8 0.0 all-gather.10.cloned.1.call-start
  35.8 9.5 %all_gather.32 = bf16[768,384]{1,0:T(8,128)(2,1)} all-gather(bf16[384,384]{1,0:T(8,128)(2,1)S(1)} %copy-done.5), channel_id=1, replica_groups=mesh['seq'=4,'wa'=2,'wb'=4] {'wa'}, dimensions={0}, use_global_device_ids=true | all-gather | bytes 884736 | tf_op jit(solution)/shard_map/all_gather | solution.py:743
  45.4 0.0 reduce-scatter.11.cloned.1.call-start
  45.6 11.0 %all-gather.1 = f32[4,6,2]{1,2,0:T(2,128)S(1)} all-gather(f32[1,6,2]{1,2,0:T(2,128)S(1)} %maximum_bitcast_fusion), channel_id=1, replica_groups=mesh['seq'=4,'wa'=2,'wb'=4] {'wb'}, dimensions={0}, use_global_device_ids=true | all-gather | bytes 240 | tf_op jit(solution)/shard_map/all_gather | solution.py:764
  56.5 0.1 reshape.99
  56.6 0.6 reshape.108.refs_2_
  57.2 0.1 broadcast_in_dim.32
  57.3 0.1 broadcast_in_dim_reshape.3
  57.4 4.4 all_gather.30
  61.8 13.5 %all-gather = bf16[4,6,768]{2,1,0:T(8,128)(2,1)S(1)} all-gather(bf16[1,6,768]{2,1,0:T(8,128)(2,1)S(1)} %bitcast.63), channel_id=1, replica_groups=mesh['seq'=4,'wa'=2,'wb'=4] {'wb'}, dimensions={0}, use_global_device_ids=true | all-gather | bytes 46080 | tf_op jit(solution)/shard_map/all_gather | solution.py:742
  75.3 0.7 pad.21.refs_6_
  76.0 6.3 all_gather.29
  82.3 0.8 copy.44
  83.1 0.1 pad.32.clone
  83.2 14.0 %all_gather.34 = f32[7,1536]{1,0:T(8,128)S(1)} all-gather(f32[7,384]{1,0:T(8,128)S(1)} %pad_maximum_fusion), channel_id=1, replica_groups=mesh['seq'=4,'wa'=2,'wb'=4] {'wb'}, dimensions={1}, use_global_device_ids=true | all-gather | bytes 53760 | tf_op jit(solution)/shard_map/all_gather | solution.py:763
  97.2 0.7 fusion.refs_8_
  98.0 30.2 %all-gather.8.cloned.1.call-done = bf16[768,2,1536]{2,0,1:T(8,128)(2,1)} async-done(((bf16[768,2,384]{2,0,1:T(8,128)(2,1)}), bf16[768,2,1536]{2,0,1:T(8,128)(2,1)}) %all-gather.8.cloned.1.call-update) | async-done | bytes 4718608 | tf_op jit(solution)/shard_map/all_gather | solution.py:740
  128.2 4.8 slice_bitcast_fusion
  132.9 45.8 %all-gather.10.cloned.1.call-done.refs_7_ = bf16[768,1536]{1,0:T(8,128)(2,1)} async-done(((bf16[768,384]{1,0:T(8,128)(2,1)}), bf16[768,1536]{1,0:T(8,128)(2,1)}) %all-gather.10.cloned.1.call-update) | async-done | bytes 2359312 | tf_op jit(solution)/shard_map/all_gather | solution.py:743
  178.8 84.2 %shard_map.262 = (bf16[512,768]{1,0:T(8,128)(2,1)}, f32[512,768]{1,0:T(8,128)}, bf16[768,1536]{1,0:T(8,128)(2,1)}, bf16[768,1536]{1,0:T(8,128)(2,1)}, bf16[768,1...) custom-call(bf16[512,768]{1,0:T(8,128)(2,1)} %bitcast.58, ...), custom_call_target="tpu_custom_call" | custom-call | tf_op jit(solution)/shard_map/pallas_call | solution.py:715
  263.0 1.9 convert_element_type.51
  264.9 0.0 reduce-scatter.15.cloned.1.call-start
  265.0 4.4 convert_element_type.52
  269.5 0.0 reduce-scatter.7.cloned.1.call-start
  269.5 1.6 copy-done
  271.1 5.9 maximum_convert_fusion
  277.0 0.0 all-reduce.13.cloned.1.call-start
  277.1 7.7 reduce-scatter.11.cloned.1.call-done
  284.9 62.2 %reduce-scatter.15.cloned.1.call-done = f32[384,1536]{1,0:T(8,128)} async-done(((f32[768,1536]{1,0:T(8,128)}), f32[384,1536]{1,0:T(8,128)}) %reduce-scatter.15.cloned.1.call-update) | async-done | bytes 2359312 | tf_op jit(solution)/shard_map/reduce_scatter | solution.py:788
  347.2 112.7 %reduce-scatter.7.cloned.1.call-done = f32[384,2,1536]{2,0,1:T(8,128)} async-done(((f32[768,2,1536]{2,0,1:T(8,128)}), f32[384,2,1536]{2,0,1:T(8,128)}) %reduce-scatter.7.cloned.1.call-update) | async-done | bytes 4718608 | tf_op jit(solution)/shard_map/reduce_scatter | solution.py:788
  459.9 0.5 all-reduce.11.cloned.1.call-update
  460.5 0.3 copy-done.7
  460.9 0.6 reshape.104
  461.5 0.0 all-reduce.15.cloned.1.call-start
  461.6 37.7 %all-reduce.13.cloned.1.call-done = f32[384,256]{1,0:T(8,128)} async-done(((f32[384,256]{1,0:T(8,128)}), f32[384,256]{1,0:T(8,128)}) %all-reduce.13.cloned.1.call-update) | async-done | bytes 393232 | tf_op jit(solution)/shard_map/psum | solution.py:792
  499.3 1.9 reshape.102
  501.2 48.1 %reduce-scatter.17.cloned.1.call-done = f32[384,384]{1,0:T(8,128)} async-done(((f32[384,1536]{1,0:T(8,128)}), f32[384,384]{1,0:T(8,128)}) %reduce-scatter.17.cloned.1.call-update) | async-done | bytes 589840 | tf_op jit(solution)/shard_map/reduce_scatter | solution.py:790
  549.4 87.2 %reduce-scatter.9.cloned.1.call-done = f32[384,2,384]{2,0,1:T(8,128)} async-done(((f32[384,2,1536]{2,0,1:T(8,128)}), f32[384,2,384]{2,0,1:T(8,128)}) %reduce-scatter.9.cloned.1.call-update) | async-done | bytes 1179664 | tf_op jit(solution)/shard_map/reduce_scatter | solution.py:790
  636.6 0.6 dynamic-slice
  637.9 126.2 %all-reduce.11.cloned.1.call-done = f32[16,1792]{1,0:T(8,128)} async-done(((f32[16,1792]{1,0:T(8,128)}), f32[16,1792]{1,0:T(8,128)}) %all-reduce.11.cloned.1.call-update) | async-done | bytes 114704 | tf_op jit(solution)/shard_map/psum | solution.py:799
  764.1 0.7 slice_bitcast_fusion.2
  764.8 0.1 reshape.106
  764.9 0.1 reshape.107
  765.0 0.7 slice.73
  765.7 0.6 reshape.105
  766.3 1.3 slice.74
  767.6 0.9 slice.72
  768.5 0.7 dynamic-slice_reduce_fusion
  769.2 0.1 constant_dynamic-slice_fusion.2
  769.2 0.6 constant_dynamic-slice_fusion.1
  769.8 1.3 slice_reduce_fusion
  771.2 0.5 slice_bitcast_fusion.3
  771.7 6.0 reduce-scatter.13.cloned.1.call-done
  777.7 19.9 %all-reduce.5 = f32[384,24]{0,1:T(8,128)S(1)} all-reduce(f32[384,24]{0,1:T(8,128)} %reduce-scatter.13.cloned.1.call-done), channel_id=6, replica_groups=mesh['seq'=4,'wa'=2,'wb'=4] {'wb'}, use_global_device_ids=true, to_apply=%region_8.9.clone | all-reduce | flops 9216 | bytes 73728
  797.6 11.6 %psum.46 = f32[384,6]{0,1:T(8,128)} all-reduce(f32[384,6]{0,1:T(8,128)S(1)} %constant_dynamic-slice_fusion), channel_id=1, replica_groups=mesh['seq'=4,'wa'=2,'wb'=4] {'seq'}, use_global_device_ids=true, to_apply=%region_9.10 | all-reduce | flops 2304 | bytes 18432 | tf_op jit(solution)/shard_map/psum | solution.py:793
  809.2 24.7 %all-reduce.15.cloned.1.call-done = (f32[384,2,384]{2,0,1:T(8,128)}, f32[384,2,128]{2,1,0:T(2,128)}, f32[384,384]{1,0:T(8,128)}) async-done(((f32[384,2,384]{2,0,1:T(8,128)}, f32[384,2,128]{2,1,0:T(2,128)}, f32[384,384]{1,0:T(8,128)}), (f32[384,2,384]{2,0,1:T(8,128)}, f32[384,2,128]{2,1,0:T(2,128)}, f32[384,384]{1,0:T(8,128)})) %all-reduce.15.cloned.1.call-update) | async-done | bytes 2162704 | tf_op jit(solution)/shard_map/psum | solution.py:793
  833.9 3.2 copy.38
  837.1 0.9 copy.53
  838.0 1.1 copy.54
  839.2 0.7 copy.55
  839.9 0.8 copy.56
  (69 shorter events, 0.6 us)
Async XLA Ops:
  7.2 28.7 %copy-start.5 = (bf16[384,384]{1,0:T(8,128)(2,1)S(1)}, bf16[384,384]{1,0:T(8,128)(2,1)}, u32[]{:S(2)}) copy-start(bf16[384,384]{1,0:T(8,128)(2,1)} %param.29) | copy-start | bytes 884740
  7.2 38.3 %copy-start.17 = (bf16[2,128]{1,0:T(2,128)(2,1)S(1)}, bf16[2,128]{1,0:T(2,128)(2,1)}, u32[]{:S(2)}) copy-start(bf16[2,128]{1,0:T(2,128)(2,1)} %param.24) | copy-start | bytes 1540
  7.2 38.3 %copy-start.12 = (bf16[384]{0:T(512)(128)(2,1)S(1)}, bf16[384]{0:T(512)(128)(2,1)}, u32[]{:S(2)}) copy-start(bf16[384]{0:T(512)(128)(2,1)} %param.22) | copy-start | bytes 2308
  7.2 38.3 %copy-start.13 = (bf16[384]{0:T(512)(128)(2,1)S(1)}, bf16[384]{0:T(512)(128)(2,1)}, u32[]{:S(2)}) copy-start(bf16[384]{0:T(512)(128)(2,1)} %param.28) | copy-start | bytes 2308
  7.2 38.3 %copy-start.15 = (f32[6]{0:T(128)S(1)}, f32[6]{0:T(128)}, u32[]{:S(2)}) copy-start(f32[6]{0:T(128)} %param.26) | copy-start | bytes 76
  7.2 38.3 %copy-start.16 = (f32[6]{0:T(128)S(1)}, f32[6]{0:T(128)}, u32[]{:S(2)}) copy-start(f32[6]{0:T(128)} %param.25) | copy-start | bytes 76
  7.2 49.4 %copy-start.11 = (bf16[768]{0:T(1024)(128)(2,1)S(1)}, bf16[768]{0:T(1024)(128)(2,1)}, u32[]{:S(2)}) copy-start(bf16[768]{0:T(1024)(128)(2,1)} %param.17) | copy-start | bytes 4612
  7.3 50.0 %copy-start.10 = (bf16[4,2,128]{2,1,0:T(2,128)(2,1)S(1)}, bf16[4,2,128]{2,1,0:T(2,128)(2,1)}, u32[]{:S(2)}) copy-start(bf16[4,2,128]{2,1,0:T(2,128)(2,1)} %param.23) | copy-start | bytes 6148
  7.3 50.0 %copy-start.14 = (f32[6]{0:T(128)S(1)}, f32[6]{0:T(128)}, u32[]{:S(2)}) copy-start(f32[6]{0:T(128)} %param.27) | copy-start | bytes 76
  7.3 50.1 %copy-start.9 = (bf16[4,384]{1,0:T(4,128)(2,1)S(1)}, bf16[4,384]{1,0:T(4,128)(2,1)}, u32[]{:S(2)}) copy-start(bf16[4,384]{1,0:T(4,128)(2,1)} %param.21) | copy-start | bytes 9220
  7.3 50.1 %copy-start.8 = (bf16[384,6]{0,1:T(8,128)(2,1)S(1)}, bf16[384,6]{0,1:T(8,128)(2,1)}, u32[]{:S(2)}) copy-start(bf16[384,6]{0,1:T(8,128)(2,1)} %param.20) | copy-start | bytes 13828
  7.3 68.7 %copy-start.6 = (bf16[384,2,128]{2,1,0:T(2,128)(2,1)S(1)}, bf16[384,2,128]{2,1,0:T(2,128)(2,1)}, u32[]{:S(2)}) copy-start(bf16[384,2,128]{2,1,0:T(2,128)(2,1)} %param.19) | copy-start | bytes 589828
  7.3 28.5 %all-gather.6.cloned.1.call-start = ((), (), s32[]{:S(2)}) async-start(), calls=%async_computation.6 | async-start | bytes 1769472 | tf_op jit(solution)/shard_map/all_gather | solution.py:740
  9.5 118.7 %all-gather.8.cloned.1.call-start = ((), (), s32[]{:S(2)}) async-start(), calls=%async_computation.7 | async-start | bytes 5898240 | tf_op jit(solution)/shard_map/all_gather | solution.py:740
  35.8 143.0 %all-gather.10.cloned.1.call-start = ((), (), s32[]{:S(2)}) async-start(), calls=%async_computation.8 | async-start | bytes 2949120 | tf_op jit(solution)/shard_map/all_gather | solution.py:743
  45.4 239.4 %reduce-scatter.11.cloned.1.call-start = ((), (), s32[]{:S(2)}) async-start(), calls=%async_computation.12 | async-start | bytes 1179648 | tf_op jit(solution)/shard_map/reduce_scatter | solution.py:788
  264.9 82.2 %reduce-scatter.15.cloned.1.call-start = ((), (), s32[]{:S(2)}) async-start(), calls=%async_computation.15 | async-start | bytes 7077888 | tf_op jit(solution)/shard_map/reduce_scatter | solution.py:788
  269.4 1.7 copy-start
  269.5 190.4 %reduce-scatter.7.cloned.1.call-start = ((), (), s32[]{:S(2)}) async-start(), calls=%async_computation.10 | async-start | bytes 14155776 | tf_op jit(solution)/shard_map/reduce_scatter | solution.py:788
  277.0 222.2 %all-reduce.13.cloned.1.call-start = ((), (), s32[]{:S(2)}) async-start(), calls=%async_computation.13 | async-start | bytes 786432 | tf_op jit(solution)/shard_map/psum | solution.py:792
  284.8 264.5 %reduce-scatter.17.cloned.1.call-start = ((), (), s32[]{:S(2)}) async-start(), calls=%async_computation.16 | async-start | bytes 2949120 | tf_op jit(solution)/shard_map/reduce_scatter | solution.py:790
  347.1 289.5 %reduce-scatter.9.cloned.1.call-start = ((), (), s32[]{:S(2)}) async-start(), calls=%async_computation.11 | async-start | bytes 5898240 | tf_op jit(solution)/shard_map/reduce_scatter | solution.py:790
  459.8 1.0 copy-start.7
  459.9 176.8 %copy-start.18 = (u32[32]{0:T(128)S(1)}, u32[32]{0:T(128)}, u32[]{:S(2)}) copy-start(u32[32]{0:T(128)} %constant.38) | copy-start | bytes 388
  459.9 304.3 %all-reduce.11.cloned.1.call-start = ((), (), s32[]{:S(2)}) async-start(), calls=%async_computation.9 | async-start | bytes 229376 | tf_op jit(solution)/shard_map/psum | solution.py:799
  460.5 317.2 %reduce-scatter.13.cloned.1.call-start = ((), (), s32[]{:S(2)}) async-start(), calls=%async_computation.14 | async-start | bytes 110592 | tf_op jit(solution)/shard_map/reduce_scatter | solution.py:788
  461.5 372.4 %all-reduce.15.cloned.1.call-start = ((), (), s32[]{:S(2)}) async-start(), calls=%async_computation.17 | async-start | bytes 4325376 | tf_op jit(solution)/shard_map/psum | solution.py:793
  636.6 200.6 %copy-start.2 = (bf16[512,768]{1,0:T(8,128)(2,1)S(1)}, bf16[512,768]{1,0:T(8,128)(2,1)}, u32[]{:S(2)}) copy-start(bf16[512,768]{1,0:T(8,128)(2,1)} %get-tuple-element.23) | copy-start | bytes 2359300
  636.6 201.4 %copy-start.1 = (f32[512,768]{1,0:T(8,128)S(1)}, f32[512,768]{1,0:T(8,128)}, u32[]{:S(2)}) copy-start(f32[512,768]{1,0:T(8,128)} %get-tuple-element.24) | copy-start | bytes 4718596
  837.1 2.0 copy-start.4
  838.0 1.9 copy-start.3
Sparse Core Ops, SparseCore 0:
  10.3 25.4 all-gather.5
  37.4 90.7 all-gather.7
  129.8 48.9 all-gather.9
  265.1 19.7 reduce-scatter.10
  287.1 59.9 reduce-scatter.14
  349.2 110.5 reduce-scatter.6
  462.2 37.0 all-reduce.12
  501.7 47.6 reduce-scatter.16
  551.8 84.7 reduce-scatter.8
  642.9 121.1 all-reduce.10
  767.0 10.6 reduce-scatter.12
  780.8 53.0 all-reduce.14
